TPU v7x, 256 devices: a whole 4x4x8 slice. The times are simulated.
256 devices in a mesh: patch: 32 (over y_lo, z, core), tensor: 8 (over y_hi, x).
Axes of the slice: x: 4, y: 4 (y_hi: 2, y_lo: 2; y = y_hi * 2 + y_lo), z: 8, core: 2. Of those that a mesh axis runs over, the one named last changes fastest.
Arguments:
- tokens: bfloat16 [8192, 3072], P('patch', 'tensor'), may hold values from -6 to 6
- shift: float32 [3072], replicated, may hold values from -3 to 3
- scale: float32 [3072], replicated, may hold values from -0.9 to 0.9
- gate: float32 [3072], P('tensor'), may hold values from 0.5 to 1.5
- w_qkv: bfloat16 [3072, 3, 3072], P(None, None, 'tensor'), may hold values from -0.109375 to 0.109375
- w_out: bfloat16 [3072, 3072], P('tensor'), may hold values from -0.109375 to 0.109375
- stale_keys: bfloat16 [8192, 3072], P('patch', 'tensor'), may hold values from -180 to 180
- stale_values: bfloat16 [8192, 3072], P('patch', 'tensor'), may hold values from -6 to 6
Outputs:
- mixed: bfloat16 [8192, 3072], P('patch', 'tensor')
- branch: float32 [8192, 3072], P('patch', 'tensor')
All inputs are finite; a program needn't handle non-finite values.
Results may differ from a plain program's by a relative error of at most 0.017.
The roundings to bfloat16 on the way count: a program that leaves them out, or rounds other values in their place, can miss the bound.
Values may be sent and summed in bfloat16 or wider, within the bound.
A program may use at most 128 MiB of HBM per device.

v0:
```python
import jax
import jax.numpy as jnp
from jax import lax
from jax.sharding import PartitionSpec as P

HD = 128


def local(tokens, shift, scale, gate, w_qkv, w_out, stale_keys, stale_values):
    tok_rows = tokens.shape[0]
    whole = lax.all_gather(tokens, "tensor", axis=1, tiled=True).astype(jnp.float32)
    center = jnp.mean(whole, axis=1, keepdims=True)
    spread = jnp.mean((whole - center) ** 2, axis=1, keepdims=True)
    normed = (whole - center) * lax.rsqrt(spread + 1e-06)
    modulated = (normed * (1.0 + scale) + shift).astype(jnp.bfloat16)
    width = w_qkv.shape[2]
    heads_local = width // HD
    qkv = jnp.dot(
        modulated, w_qkv.reshape(w_qkv.shape[0], 3 * width), preferred_element_type=jnp.float32
    ).astype(jnp.bfloat16)
    query = qkv[:, :width].reshape(tok_rows, heads_local, HD)
    fresh_keys = qkv[:, width : 2 * width]
    fresh_values = qkv[:, 2 * width :]
    inv_root = 1.0 / jnp.sqrt(jnp.float32(HD))
    patch_index = lax.axis_index("patch")
    all_keys, all_values = (
        lax.all_gather(stale_keys, "patch", axis=0, tiled=True),
        lax.all_gather(stale_values, "patch", axis=0, tiled=True),
    )
    offset = patch_index * tok_rows
    zero_col = jnp.zeros((), jnp.int32)
    all_keys = lax.dynamic_update_slice(all_keys, fresh_keys, (offset, zero_col))
    all_values = lax.dynamic_update_slice(all_values, fresh_values, (offset, zero_col))
    shaped = all_keys.reshape(all_keys.shape[0], heads_local, HD)
    score = jnp.einsum("thd,uhd->htu", query, shaped, preferred_element_type=jnp.float32) * inv_root
    highest = jnp.max(score, axis=-1, keepdims=True)
    expo = jnp.exp(score - highest)
    total = jnp.sum(expo, axis=-1, keepdims=True)
    shaped = all_values.reshape(all_values.shape[0], heads_local, HD)
    accum = jnp.einsum(
        "htu,uhd->htd", expo.astype(jnp.bfloat16), shaped, preferred_element_type=jnp.float32
    )
    attended = (accum / total).astype(jnp.bfloat16).transpose(1, 0, 2).reshape(tok_rows, width)
    partial_sum = jnp.dot(attended, w_out, preferred_element_type=jnp.float32)
    summed = lax.psum(partial_sum.astype(jnp.bfloat16), "tensor").astype(jnp.float32)
    share_width = gate.shape[0]
    share = lax.dynamic_slice_in_dim(summed, lax.axis_index("tensor") * share_width, share_width, 1)
    branch = gate * share
    return ((tokens.astype(jnp.float32) + branch).astype(jnp.bfloat16), branch)


def solution(mesh):
    in_specs = (
        P("patch", "tensor"),
        P(),
        P(),
        P("tensor"),
        P(None, None, "tensor"),
        P("tensor", None),
        P("patch", "tensor"),
        P("patch", "tensor"),
    )
    out_specs = (P("patch", "tensor"), P("patch", "tensor"))
    return jax.shard_map(local, mesh=mesh, in_specs=in_specs, out_specs=out_specs, check_vma=False)
```

profile of v0, /device:TPU:2, one launch (start us, length us, event | category | flops | bytes accessed | tf_op | source)
XLA Modules:
  0.0 372.4 jit_solution(9787576197364196367)
XLA Ops:
  7.2 0.0 copy-start
  7.2 0.0 all-gather.4.cloned.1.call-start
  7.2 0.7 all-gather.4.cloned.1.call-update
  7.9 0.0 all-gather.6.cloned.1.call-start
  8.0 1.7 copy.15
  9.7 0.0 all-gather.6.cloned.1.call-update
  9.7 0.0 all-gather.8.cloned.1.call-start
  9.8 1.7 copy.19
  11.5 0.0 all-gather.8.cloned.1.call-update
  11.5 0.0 all-reduce.2.cloned.1.call-start
  11.6 0.0 copy-start.2
  11.6 0.0 copy-start.4
  11.6 10.3 %copy.13 = bf16[3072,3,384]{0,2,1:T(8,128)(2,1)} copy(bf16[3072,3,384]{2,0,1:T(8,128)(2,1)} %param.12) | data formatting | bytes 14155776 | tf_op args[4]
  21.9 49.0 %all-gather.4.cloned.1.call-done = bf16[256,3072]{1,0:T(8,128)(2,1)} async-done(((bf16[256,384]{1,0:T(8,128)(2,1)}), bf16[256,3072]{1,0:T(8,128)(2,1)}) %all-gather.4.cloned.1.call-update) | async-done | bytes 1572880 | tf_op jit(solution)/shard_map/all_gather | solution.py:11
  70.9 1.7 convert_reduce_fusion
  72.6 2.0 fusion.8
  74.6 5.9 %convolution_convert_fusion.1 = bf16[256,1152]{1,0:T(8,128)(2,1)S(1)} fusion(bf16[3072,1152]{0,1:T(8,128)(2,1)} %bitcast.18, bf16[256,3072]{1,0:T(8,128)(2,1)} %all-gather.4.cloned.1.call-done, f32[3072]{0:T(1024)S(1)} %copy-done.4, f32[3072]{0:T(1024)S(1)} %broadcast_add_fusion, f32[256]{0:T(256)S(1)} %add_rsqrt_fusion, f32[256]{0:T(256)S(1)} %broadcast_multiply_fusion), kind=kOutput, calls=%fused_computation.16 | convolution fusion | flops 1816952832 | bytes 9267200 | tf_op jit(solution)/shard_map/dot_general | solution.py:18
  80.6 0.1 fusion.27
  80.6 0.1 copy.16
  80.8 0.1 copy.20
  80.9 0.1 copy.14
  81.1 71.9 %all-gather.6.cloned.1.call-done = bf16[8192,384]{0,1:T(8,128)(2,1)} async-done(((bf16[256,384]{0,1:T(8,128)(2,1)}), bf16[8192,384]{0,1:T(8,128)(2,1)}) %all-gather.6.cloned.1.call-update) | async-done | bytes 6291472 | tf_op jit(solution)/shard_map/all_gather | solution.py:27
  153.0 81.1 %all-gather.8.cloned.1.call-done = bf16[8192,384]{0,1:T(8,128)(2,1)} async-done(((bf16[256,384]{0,1:T(8,128)(2,1)}), bf16[8192,384]{0,1:T(8,128)(2,1)}) %all-gather.8.cloned.1.call-update) | async-done | bytes 6291472 | tf_op jit(solution)/shard_map/all_gather | solution.py:28
  234.2 0.8 constant_dynamic-update-slice_fusion
  234.9 13.0 %multiply_reduce_fusion = (f32[3,256]{1,0:T(4,128)S(1)}, f32[3,256,8192]{2,1,0:T(8,128)}) fusion(bf16[256,3,128]{0,2,1:T(8,128)(2,1)S(1)} %bitcast.22, bf16[8192,3,128]{0,2,1:T(8,128)(2,1)} %bitcast.19), kind=kOutput, calls=%fused_computation.1 | convolution fusion | flops 1623194880 | bytes 31656960 | tf_op jit(solution)/shard_map/thd,uhd->htu/dot_general | solution.py:35
  247.9 10.8 %fusion = f32[3,256]{1,0:T(4,128)S(1)} fusion(f32[3,256,8192]{2,1,0:T(8,128)} %get-tuple-element.8, f32[3,256]{1,0:T(4,128)S(1)} %get-tuple-element.7), kind=kLoop, calls=%fused_computation.2 | loop fusion | flops 18873600 | bytes 25171968 | tf_op jit(solution)/shard_map/reduce_sum | solution.py:38
  258.7 0.0 copy-start.3
  258.7 12.7 %fusion.23 = bf16[256,3,128]{0,2,1:T(8,128)(2,1)S(1)} fusion(bf16[8192,3,128]{0,2,1:T(8,128)(2,1)} %bitcast.20, f32[3,256,8192]{2,1,0:T(8,128)} %get-tuple-element.8, f32[3,256]{1,0:T(4,128)S(1)} %get-tuple-element.7, f32[256,3]{0,1:T(4,128)S(1)} %bitcast.23), kind=kOutput, calls=%fused_computation.23 | convolution fusion | flops 1629683712 | bytes 31660032 | tf_op jit(solution)/shard_map/htu,uhd->htd/dot_general | solution.py:40
  271.5 2.2 convolution_convert_fusion
  273.6 0.0 all-reduce.2.cloned.1.call-update
  273.6 90.5 %all-reduce.2.cloned.1.call-done = bf16[256,3072]{1,0:T(8,128)(2,1)} async-done(((bf16[256,3072]{1,0:T(8,128)(2,1)}), bf16[256,3072]{1,0:T(8,128)(2,1)}) %all-reduce.2.cloned.1.call-update) | async-done | bytes 1572880 | tf_op jit(solution)/shard_map/psum | solution.py:45
  364.1 1.8 add_convert_fusion
  (9 shorter events, 0.0 us)
Async XLA Ops:
  7.2 264.3 %copy-start = (bf16[384,3072]{1,0:T(8,128)(2,1)S(1)}, bf16[384,3072]{1,0:T(8,128)(2,1)}, u32[]{:S(2)}) copy-start(bf16[384,3072]{1,0:T(8,128)(2,1)} %param.13) | copy-start | bytes 7077892
  7.2 63.8 %all-gather.4.cloned.1.call-start = ((), (), s32[]{:S(2)}) async-start(), calls=%async_computation | async-start | bytes 1769472 | tf_op jit(solution)/shard_map/all_gather | solution.py:11
  7.9 145.1 %all-gather.6.cloned.1.call-start = ((), (), s32[]{:S(2)}) async-start(), calls=%async_computation.1 | async-start | bytes 6488064 | tf_op jit(solution)/shard_map/all_gather | solution.py:27
  9.7 224.4 %all-gather.8.cloned.1.call-start = ((), (), s32[]{:S(2)}) async-start(), calls=%async_computation.2 | async-start | bytes 6488064 | tf_op jit(solution)/shard_map/all_gather | solution.py:28
  11.5 352.5 %all-reduce.2.cloned.1.call-start = ((), (), s32[]{:S(2)}) async-start(), calls=%async_computation.3 | async-start | bytes 3145728 | tf_op jit(solution)/shard_map/psum | solution.py:45
  11.6 10.3 %copy-start.2 = (f32[3072]{0:T(1024)S(1)}, f32[3072]{0:T(1024)}, u32[]{:S(2)}) copy-start(f32[3072]{0:T(1024)} %param.10) | copy-start | bytes 36868
  11.6 63.0 %copy-start.4 = (f32[3072]{0:T(1024)S(1)}, f32[3072]{0:T(1024)}, u32[]{:S(2)}) copy-start(f32[3072]{0:T(1024)} %param.9) | copy-start | bytes 36868
  258.7 105.4 %copy-start.1 = (bf16[256,384]{1,0:T(8,128)(2,1)S(1)}, bf16[256,384]{1,0:T(8,128)(2,1)}, u32[]{:S(2)}) copy-start(bf16[256,384]{1,0:T(8,128)(2,1)} %param.8) | copy-start | bytes 589828
  258.7 105.4 %copy-start.3 = (f32[384]{0:T(512)S(1)}, f32[384]{0:T(512)}, u32[]{:S(2)}) copy-start(f32[384]{0:T(512)} %param.11) | copy-start | bytes 4612
Sparse Core Ops, SparseCore 0:
  10.5 60.3 all-gather.3
  73.3 79.7 all-gather.5
  155.4 78.7 all-gather.7
  273.8 90.2 all-reduce.1
where the time goes:
time: 376 us; the launch traced here: 372 us
  waiting for transfers between devices  293 us (78%)
  matrix products  33.7 us (9%)
  other arithmetic  16.3 us (4%)
  local copies, waits for them, and re-layouts  15.1 us (4%)
  between operations  13.9 us (4%)
    psum x1, waiting for transfers between devices, local(): lax.psum(partial_sum.astype(jnp.bfloat16), 'tensor').astype(jnp.float32)  90.5 us
    all_gather x1, waiting for transfers between devices, local(): lax.all_gather(stale_values, 'patch', axis=0, tiled=True)  81.1 us
    all_gather x1, waiting for transfers between devices, local(): lax.all_gather(stale_keys, 'patch', axis=0, tiled=True)  71.9 us
    all_gather x1, waiting for transfers between devices, local(): lax.all_gather(tokens, 'tensor', axis=1, tiled=True).astype(jnp.float32)  49 us
    unnamed x13, local copies, waits for them, and re-layouts  13.8 us
    dot_general x1, matrix products, local(): jnp.einsum('thd,uhd->htu', query, shaped, preferred_element_type=jnp.floa...  13 us
    dot_general x1, matrix products, local(): jnp.einsum('htu,uhd->htd', expo.astype(jnp.bfloat16), shaped, preferred_e...  12.7 us
    reduce_sum x1, other arithmetic, local(): total = jnp.sum(expo, axis=-1, keepdims=True)  10.8 us
  transfers between devices with their start and end apart: 4, of which 4 were waited for; matrix products, arithmetic and copies ran while one was open for 6% of the time, Pallas kernels for 0%

commit v1 on v0

v1 whole, which is shorter than its diff:
```python
import jax
import jax.numpy as jnp
from jax import lax
from jax.experimental import pallas as pl
from jax.experimental.pallas import tpu as pltpu
from jax.sharding import PartitionSpec as P

MESH = pl.DeviceIdType.MESH
HD = 128
ROWS = 256
NH = 3
WIDTH = NH * HD
D = 3072
NT = 8
NZ = 8
LOG2E = 1.4426950408889634
EXP_SCALE = LOG2E / (HD**0.5)
DEPTH = (4, 3)
F32 = jnp.float32
BF16 = jnp.bfloat16


def dot(a, b):
    return jnp.dot(a, b, preferred_element_type=F32)


def dot_t(a, b):
    return lax.dot_general(a, b, (((0,), (0,)), ((), ())), preferred_element_type=F32)


def kernel(
    tok_in, scale_ref, shift_ref, w_in, wo_in, sk_in, sv_in,
    out_ref,
    kv, tok, mod, w, wo, att, qown, qpart, qt, fresh, m_s, l_s, acc, mean_s, dev_s,
    osend, orecv, ssend, srecv,
    loc_sem, w_sem, ring_ss, ring_rs, d2d_ss, d2d_rs, tok_ss, tok_rs, att_ss, att_rs,
    q_ss, q_rs, o_ss, o_rs, st_ss, st_rs, wo_ss, wo_rs, wx_ss, wx_rs,
):
    p, t = lax.axis_index("patch"), lax.axis_index("tensor")
    b, z, c = lax.div(p, 16), lax.rem(lax.div(p, 2), NZ), lax.rem(p, 2)
    yh, x = lax.div(t, 4), lax.rem(t, 4)

    def dev(b=b, z=z, c=c, yh=yh, x=x):
        return (b * 16 + z * 2 + c, yh * 4 + x)

    def remote(src, dst, ss, rs, to):
        return pltpu.make_async_remote_copy(
            src_ref=src, dst_ref=dst, send_sem=ss, recv_sem=rs, device_id=to, device_id_type=MESH
        )

    dz = (1 - 2 * c, 2 * c - 1)
    zs = tuple(lax.rem(z + s + NZ, NZ) for s in dz)
    sibling, partner = dev(c=1 - c), dev(b=1 - b)
    xr, xl = dev(x=lax.rem(x + 1, 4)), dev(x=lax.rem(x + 3, 4))
    yo = dev(yh=1 - yh)
    me = z * 2 + c
    qtr = b * 2 + c

    loads = [pltpu.make_async_copy(tok_in, tok.at[t], loc_sem.at[0])]
    for h in range(NH):
        cols = pl.ds(h * HD, HD)
        loads.append(pltpu.make_async_copy(sk_in.at[:, cols], kv.at[me, h, 0], loc_sem.at[1 + 2 * h]))
        loads.append(pltpu.make_async_copy(sv_in.at[:, cols], kv.at[me, h, 1], loc_sem.at[2 + 2 * h]))
    own_cols = pl.ds(pl.multiple_of(t * WIDTH, WIDTH), WIDTH)
    wo_own = pltpu.make_async_copy(wo_in.at[:, qtr, :, own_cols], wo.at[t, :, qtr], loc_sem.at[7])
    w_loads = [pltpu.make_async_copy(w_in.at[j], w.at[j], w_sem.at[j]) for j in range(3)]
    for copy in loads + w_loads + [wo_own]:
        copy.start()

    barrier = pltpu.get_barrier_semaphore()
    peers = [sibling, partner, dev(z=zs[0]), dev(z=zs[1])]
    for e in range(1, NT):
        peers.append((p, lax.rem(t + e, NT)))
    for peer in peers:
        pl.semaphore_signal(barrier, inc=1, device_id=peer, device_id_type=MESH)
    pl.semaphore_wait(barrier, len(peers))

    sent = []

    def go(make, *args):
        make(*args).start()
        sent.append((make, args))

    def slot_of(s, d):
        return lax.rem(z - d * dz[s] + NZ, NZ) * 2 + c

    def ring(s, h, d):
        slot = slot_of(s, d)
        return remote(kv.at[slot, h], kv.at[slot, h], ring_ss.at[s, h, d], ring_rs.at[s, h, d], dev(z=zs[s]))

    def share(k, h, slot):
        return remote(kv.at[slot, h], kv.at[slot, h], d2d_ss.at[k, h], d2d_rs.at[k, h], sibling)

    def own_kv(h):
        loads[1 + 2 * h].wait()
        loads[2 + 2 * h].wait()
        go(ring, 0, h, 0)
        go(ring, 1, h, 0)
        go(share, 0, h, me)

    def event(h, d):
        for s in (0, 1):
            if d > DEPTH[s]:
                continue
            slot = slot_of(s, d)
            remote(
                kv.at[slot, h], kv.at[slot, h], ring_ss.at[s, h, d - 1], ring_rs.at[s, h, d - 1], sibling
            ).wait_recv()
            if d < DEPTH[s]:
                go(ring, s, h, d)
            go(lambda s=s: share(d + 4 * s, h, slot_of(s, d)))

    slot_l, slot_r, slot_f = (yh * 4 + lax.rem(x + e, 4) for e in (3, 1, 2))
    slot_y, slot_yl, slot_yr, slot_yf = ((1 - yh) * 4 + lax.rem(x + e, 4) for e in (0, 3, 1, 2))
    upper, lower = pl.ds(0, ROWS // 2), pl.ds(ROWS // 2, ROWS // 2)

    class Gather:
        def __init__(self, buf, ss, rs):
            self.buf, self.ss, self.rs = buf, ss, rs

        def view(self, slot, rows):
            return self.buf.at[slot] if rows is None else self.buf.at[slot, rows]

        def send(self, slot, rows, to, i, j):
            go(self.copy, slot, rows, to, i, j)

        def copy(self, slot, rows, to, i, j):
            view = self.view(slot, rows)
            return remote(view, view, self.ss.at[i], self.rs.at[j], to)

        def wait(self, slot, rows, j):
            view = self.view(slot, rows)
            remote(view, view, self.ss.at[0], self.rs.at[j], sibling).wait_recv()

        def start(self):
            self.send(t, None, yo, 2, 2)
            self.send(t, None, xr, 0, 0)
            self.send(t, None, xl, 1, 1)

        def near(self):
            self.wait(slot_l, None, 0)
            self.send(slot_l, upper, xr, 3, 5)
            self.wait(slot_r, None, 1)
            self.send(slot_r, lower, xl, 4, 6)

        def across(self):
            self.wait(slot_y, None, 2)
            self.send(slot_y, None, xr, 5, 3)
            self.send(slot_y, None, xl, 6, 4)

        def far(self):
            self.wait(slot_f, upper, 5)
            self.wait(slot_f, lower, 6)

        def across_near(self):
            self.wait(slot_yl, None, 3)
            self.send(slot_yl, upper, xr, 7, 7)
            self.wait(slot_yr, None, 4)
            self.send(slot_yr, lower, xl, 8, 8)

        def across_far(self):
            self.wait(slot_yf, upper, 7)
            self.wait(slot_yf, lower, 8)

    def wo_send(e):
        to = lax.rem(t + e, NT)
        cols = pl.ds(pl.multiple_of(to * WIDTH, WIDTH), WIDTH)
        return remote(wo_in.at[:, qtr, :, cols], wo.at[t, :, qtr], wo_ss.at[e], wo_rs.at[e], (p, to))

    def wo_start():
        for e in range(1, NT):
            go(wo_send, e)

    def wo_share(i, quarter, to):
        view = wo.at[:, :, quarter]
        return remote(view, view, wx_ss.at[i], wx_rs.at[i], to)

    def wo_pass():
        for e in range(1, NT):
            frm = lax.rem(t + NT - e, NT)
            view = wo.at[frm, :, qtr]
            remote(view, view, wo_ss.at[e], wo_rs.at[e], sibling).wait_recv()
        wo_own.wait()
        go(wo_share, 0, qtr, partner)
        go(wo_share, 1, qtr, sibling)

    other = (1 - b) * 2 + c

    def wo_pass_on():
        wo_share(0, other, partner).wait_recv()
        go(wo_share, 2, other, sibling)

    def wo_end():
        wo_share(1, b * 2 + 1 - c, sibling).wait_recv()
        wo_share(2, (1 - b) * 2 + 1 - c, sibling).wait_recv()

    def stats(slot, seen):
        xb = tok[slot].astype(F32)
        mb = jnp.sum(xb, axis=1, keepdims=True) * (1.0 / WIDTH)
        cb = xb - mb
        sb = jnp.sum(cb * cb, axis=1, keepdims=True)
        if seen == 0:
            mean_s[...] = mb
            dev_s[...] = sb
        else:
            delta = mb - mean_s[...]
            mean_s[...] += delta * (1.0 / (seen + 1))
            dev_s[...] += sb + delta * delta * (WIDTH * seen / (seen + 1))

    def finish_block(h, halves, first):
        top = halves[0][0].max(axis=0, keepdims=True)
        for s, _ in halves[1:]:
            top = jnp.maximum(top, s.max(axis=0, keepdims=True))
        if first:
            new = top
        else:
            old = m_s[h]
            new = jnp.maximum(old, top)
            alpha = jnp.exp2((old - new) * EXP_SCALE)
        m_s[h] = new
        shift_by = new * EXP_SCALE
        total, summed = None, None
        for s, times in halves:
            weights = jnp.exp2(s * EXP_SCALE - shift_by)
            part = jnp.sum(weights, axis=0, keepdims=True)
            prod = times(weights.astype(BF16))
            total = part if total is None else total + part
            summed = prod if summed is None else summed + prod
        if first:
            l_s[h] = total
            acc[h] = summed
        else:
            l_s[h] = l_s[h] * alpha + total
            acc[h] = acc[h] * alpha + summed

    def first_block(h):
        remote(
            kv.at[me, h], kv.at[me, h], d2d_ss.at[0, h], d2d_rs.at[0, h], sibling
        ).wait_recv()
        near = z * 2 + 1 - c
        query = qt[h]
        mine, theirs = query[:, :ROWS], query[:, ROWS:]
        s0 = jnp.concatenate([dot(fresh[h, 0], mine), dot(kv[me, h, 0], theirs)], axis=1)
        s1 = dot(kv[near, h, 0], query)

        def times0(weights):
            return jnp.concatenate(
                [dot_t(fresh[h, 1], weights[:, :ROWS]), dot_t(kv[me, h, 1], weights[:, ROWS:])], axis=1
            )

        finish_block(h, [(s0, times0), (s1, lambda weights: dot_t(kv[near, h, 1], weights))], True)

    def later_block(h, i):
        d = lax.div(i - 1, 2) + 1
        side = lax.rem(i - 1, 2)
        k = d + 4 * (1 - side) * (1 - lax.div(d, 4))
        chip = lax.rem(z - d * dz[0] * (1 - 2 * side) + NZ, NZ)
        slot = chip * 2 + 1 - c
        remote(
            kv.at[slot, h], kv.at[slot, h], d2d_ss.at[k, h], d2d_rs.at[k, h], sibling
        ).wait_recv()
        query = qt[h]
        halves = []
        for i in (0, 1):
            slot = chip * 2 + i
            s = dot(kv[slot, h, 0], query)
            halves.append((s, lambda weights, slot=slot: dot_t(kv[slot, h, 1], weights)))
        finish_block(h, halves, False)

    gathers = [Gather(att.at[h], att_ss.at[h], att_rs.at[h]) for h in range(NH)]

    def o_copy(h):
        return remote(osend.at[h], orecv.at[h], o_ss.at[h], o_rs.at[h], partner)

    def s_copy(h):
        return remote(ssend.at[h], srecv.at[h], st_ss.at[h], st_rs.at[h], partner)

    def q_copy(h):
        return remote(qown.at[h], qpart.at[h], q_ss.at[h], q_rs.at[h], partner)

    def give(h):
        total = l_s[h, :, ROWS:]
        osend[h] = (acc[h, :, ROWS:] / total).astype(BF16)
        ssend[h, 0:1, :] = m_s[h, :, ROWS:]
        ssend[h, 1:2, :] = total
        go(o_copy, h)
        go(s_copy, h)

    def merge(h):
        o_copy(h).wait_recv()
        s_copy(h).wait_recv()
        m1, m2 = m_s[h, :, :ROWS], srecv[h, 0:1, :]
        top = jnp.maximum(m1, m2)
        w1 = jnp.exp2((m1 - top) * EXP_SCALE)
        w2 = jnp.exp2((m2 - top) * EXP_SCALE) * srecv[h, 1:2, :]
        inv = 1.0 / (l_s[h, :, :ROWS] * w1 + w2)
        attended = acc[h, :, :ROWS] * (w1 * inv) + orecv[h].astype(F32) * (w2 * inv)
        att[h, t] = attended.T.astype(BF16)
        gathers[h].start()

    def project(h):
        total = None
        for s in range(0, NT, 2):
            lhs = jnp.concatenate([att[h, s], att[h, s + 1]], axis=1)
            rhs = jnp.concatenate(
                [wo[s, h].reshape(HD, WIDTH), wo[s + 1, h].reshape(HD, WIDTH)], axis=0
            )
            part = dot(lhs, rhs)
            total = part if total is None else total + part
        if h == 0:
            out_ref[...] = total
        else:
            out_ref[...] += total

    own_kv(0)
    loads[0].wait()
    tg = Gather(tok, tok_ss, tok_rs)
    tg.start()
    own_kv(1)
    stats(t, 0)
    event(0, 1)
    own_kv(2)
    tg.near()
    tg.across()
    stats(slot_l, 1)
    stats(slot_r, 2)
    event(0, 2)
    stats(slot_y, 3)
    event(1, 1)
    tg.far()
    stats(slot_f, 4)
    tg.across_near()
    stats(slot_yl, 5)
    stats(slot_yr, 6)
    event(0, 3)
    tg.across_far()
    wo_start()
    stats(slot_yf, 7)
    event(1, 2)
    mean = mean_s[...]
    inv = lax.rsqrt(dev_s[...] * (1.0 / D) + 1e-6)
    for i in range(NT):
        cols = slice(i * WIDTH, (i + 1) * WIDTH)
        normed = (tok[i].astype(F32) - mean) * inv
        mod[:, cols] = (normed * (1.0 + scale_ref[:, cols]) + shift_ref[:, cols]).astype(BF16)
    event(2, 1)
    for j in range(3):
        w_loads[j].wait()
        res = dot(mod[...], w[j]).astype(BF16)
        for h in range(NH):
            head = res[:, h * HD : (h + 1) * HD]
            if j == 0:
                qown[h] = head
                go(q_copy, h)
                qt[h, :, :ROWS] = head.T
            else:
                fresh[h, j - 1] = head
        if j == 0:
            event(0, 4)
        if j == 1:
            event(1, 3)
    for h in range(NH):
        q_copy(h).wait_recv()
        qt[h, :, ROWS:] = qpart[h].T

    plan = {
        2: [lambda: event(2, 2)],
        4: [lambda: event(1, 4)],
        5: [wo_pass],
        8: [lambda: give(0)],
        9: [lambda: event(2, 3)],
        11: [lambda: merge(0)],
        12: [wo_pass_on],
        13: [lambda: event(2, 4)],
        14: [lambda: gathers[0].near(), lambda: gathers[0].across()],
        16: [lambda: give(1)],
        17: [lambda: gathers[0].across_near()],
        19: [lambda: merge(1)],
        20: [lambda: gathers[0].far(), lambda: gathers[0].across_far()],
        22: [lambda: gathers[1].near(), lambda: gathers[1].across()],
    }

    def step(n, _):
        for at, todo in plan.items():

            @pl.when(n == at)
            def _(todo=todo):
                for f in todo:
                    f()

        h, i = lax.div(n, 8), lax.rem(n, 8)

        @pl.when(i == 0)
        def _():
            first_block(h)

        @pl.when(i > 0)
        def _():
            later_block(h, i)

        return 0

    lax.fori_loop(0, 8 * NH, step, 0)
    give(2)
    gathers[1].across_near()
    wo_end()
    merge(2)
    project(0)
    gathers[2].near()
    gathers[2].across()
    gathers[1].far()
    gathers[1].across_far()
    project(1)
    gathers[2].across_near()
    gathers[2].far()
    gathers[2].across_far()
    project(2)
    for make, args in sent:
        make(*args).wait_send()


def block(tokens, scale, shift, w, wo, sk, sv):
    dma, vmem = pltpu.SemaphoreType.DMA, pltpu.VMEM
    anywhere = pl.BlockSpec(memory_space=pl.ANY)
    inside = pl.BlockSpec(memory_space=pltpu.VMEM)
    return pl.pallas_call(
        kernel,
        out_shape=jax.ShapeDtypeStruct((ROWS, WIDTH), F32),
        in_specs=[anywhere, inside, inside, anywhere, anywhere, anywhere, anywhere],
        out_specs=inside,
        scratch_shapes=[
            vmem((2 * NZ, NH, 2, ROWS, HD), BF16),
            vmem((NT, ROWS, WIDTH), BF16),
            vmem((ROWS, D), BF16),
            vmem((3, D, WIDTH), BF16),
            vmem((NT, NH, 4, 32, WIDTH), BF16),
            vmem((NH, NT, ROWS, HD), BF16),
            vmem((NH, ROWS, HD), BF16),
            vmem((NH, ROWS, HD), BF16),
            vmem((NH, HD, 2 * ROWS), BF16),
            vmem((NH, 2, ROWS, HD), BF16),
            vmem((NH, 1, 2 * ROWS), F32),
            vmem((NH, 1, 2 * ROWS), F32),
            vmem((NH, HD, 2 * ROWS), F32),
            vmem((ROWS, 1), F32),
            vmem((ROWS, 1), F32),
            vmem((NH, HD, ROWS), BF16),
            vmem((NH, HD, ROWS), BF16),
            vmem((NH, 8, ROWS), F32),
            vmem((NH, 8, ROWS), F32),
            dma((8,)),
            dma((3,)),
            dma((2, NH, 4)),
            dma((2, NH, 4)),
            dma((8, NH)),
            dma((8, NH)),
            dma((9,)),
            dma((9,)),
            dma((NH, 9)),
            dma((NH, 9)),
            dma((NH,)),
            dma((NH,)),
            dma((NH,)),
            dma((NH,)),
            dma((NH,)),
            dma((NH,)),
            dma((NT,)),
            dma((NT,)),
            dma((3,)),
            dma((3,)),
        ],
        compiler_params=pltpu.CompilerParams(
            collective_id=0, has_side_effects=True, vmem_limit_bytes=56 * 1024 * 1024
        ),
        name="attention_block",
    )(tokens, scale, shift, w, wo, sk, sv)


def local(tokens, shift, scale, gate, w_qkv, w_out, stale_keys, stale_values):
    summed = block(
        tokens,
        scale.reshape(1, D),
        shift.reshape(1, D),
        jnp.transpose(w_qkv, (1, 0, 2)),
        w_out.reshape(NH, 4, 32, D),
        stale_keys,
        stale_values,
    )
    branch = gate * summed
    return ((tokens.astype(F32) + branch).astype(BF16), branch)


def solution(mesh):
    in_specs = (
        P("patch", "tensor"),
        P(),
        P(),
        P("tensor"),
        P(None, None, "tensor"),
        P("tensor", None),
        P("patch", "tensor"),
        P("patch", "tensor"),
    )
    out_specs = (P("patch", "tensor"), P("patch", "tensor"))
    return jax.shard_map(local, mesh=mesh, in_specs=in_specs, out_specs=out_specs, check_vma=False)
```

time: 376 us -> 95.7 us (0.25)
  waiting for transfers between devices: 293 us -> 0 us
  Pallas kernels: 0 us -> 93 us
  matrix products: 33.7 us -> 0 us
  local copies, waits for them, and re-layouts: 15.1 us -> 0.01 us
  other arithmetic: 16.3 us -> 1.85 us
  between operations: 13.9 us -> 0.67 us
    all_gather x3 -> x0, waiting for transfers between devices: 202 us -> none  [the longest x1 81.1 us: local(): lax.all_gather(stale_values, 'patch', axis=0, tiled=True)]
    pallas_call x0 -> x1, Pallas kernels: none -> 93 us  [block(): pl.pallas_call(kernel, out_shape=jax.ShapeDtypeStruct((ROWS, WIDTH), F32)...]
    psum x1 -> x0, waiting for transfers between devices: 90.5 us -> none  [local(): lax.psum(partial_sum.astype(jnp.bfloat16), 'tensor').astype(jnp.float32)]
    dot_general x4 -> x0, matrix products: 33.7 us -> none  [the longest x1 13 us: local(): jnp.einsum('thd,uhd->htu', query, shaped, preferred_element_type=jnp.floa...]
    reduce_sum x3 -> x0, other arithmetic: 14.5 us -> none  [the longest x1 10.8 us: local(): total = jnp.sum(expo, axis=-1, keepdims=True)]
    unnamed x13 -> x4, local copies, waits for them, and re-layouts: 13.8 us -> 0.01 us
  transfers between devices with their start and end apart: 4 -> 0, of which waited for: 4 -> 0; matrix products, arithmetic and copies ran while one was open for 6% -> 0% of each run, Pallas kernels for 0% -> 0%
where the time goes in v1:
time: 95.7 us; the launch traced here: 95.5 us
  Pallas kernels  93 us (97%)
  other arithmetic  1.85 us (2%)
    pallas_call x1, Pallas kernels, block(): pl.pallas_call(kernel, out_shape=jax.ShapeDtypeStruct((ROWS, WIDTH), F32)...  93 us

profile of v1, /device:TPU:2, one launch (start us, length us, event | category | flops | bytes accessed | tf_op | source)
XLA Modules:
  0.0 95.5 jit_solution(7728375816025870571)
XLA Ops:
  0.6 0.0 copy-start
  0.6 0.0 copy-start.1
  0.7 93.0 %attention_block.1 = f32[256,384]{1,0:T(8,128)} custom-call(bf16[256,384]{1,0:T(8,128)(2,1)} %tok_in.1, f32[1,3072]{1,0:T(1,128)} %bitcast.6, f32[1,3072]{1,0:T(1,128)} %bitcast.7, bf16[3,3072,384]{2,1,0:T(8,128)(2,1)} %bitcast.4, bf16[3,4,32,3072]{3,2,1,0:T(8,128)(2,1)} %bitcast.5, bf16[256,384]{1,0:T(8,128)(2,1)} %sk_in.1, bf16[256,384]{1,0:T(8,128)(2,1)} %sv_in.1), custom_call_target="tpu_custom_call" | custom-call | tf_op jit(solution)/shard_map/attention_block/pallas_call | solution.py:426
  93.7 0.0 copy-done
  93.7 0.0 copy-done.1
  93.7 1.9 %add_convert_fusion = (bf16[256,384]{1,0:T(8,128)(2,1)}, f32[256,384]{1,0:T(8,128)}) fusion(bf16[256,384]{1,0:T(8,128)(2,1)S(1)} %copy-done, f32[256,384]{1,0:T(8,128)} %attention_block.1, f32[384]{0:T(512)S(1)} %copy-done.1), kind=kLoop, calls=%fused_computation | loop fusion | flops 393216 | bytes 1181184 | tf_op jit(solution)/shard_map/convert_element_type | solution.py:490
Async XLA Ops:
  0.6 93.0 %copy-start = (bf16[256,384]{1,0:T(8,128)(2,1)S(1)}, bf16[256,384]{1,0:T(8,128)(2,1)}, u32[]{:S(2)}) copy-start(bf16[256,384]{1,0:T(8,128)(2,1)} %tok_in.1) | copy-start | bytes 589828
  0.6 93.0 %copy-start.1 = (f32[384]{0:T(512)S(1)}, f32[384]{0:T(512)}, u32[]{:S(2)}) copy-start(f32[384]{0:T(512)} %param.11) | copy-start | bytes 4612

commit v2 on v1

v2 whole, which is shorter than its diff:
```python
import jax
import jax.numpy as jnp
from jax import lax
from jax.experimental import pallas as pl
from jax.experimental.pallas import tpu as pltpu
from jax.sharding import PartitionSpec as P

MESH = pl.DeviceIdType.MESH
HD = 128
ROWS = 256
NH = 3
WIDTH = NH * HD
D = 3072
NT = 8
NZ = 8
LOG2E = 1.4426950408889634
EXP_SCALE = LOG2E / (HD**0.5)
DEPTH = (4, 3)
FRESH = 2 * NZ
F32 = jnp.float32
BF16 = jnp.bfloat16


def dot(a, b):
    return jnp.dot(a, b, preferred_element_type=F32)


def kernel(
    tok_in, scale_ref, shift_ref, w_in, wo_in, sk_in, sv_in,
    out_ref,
    kv, vtmp, tok, mod, w, wo, wo2, att, att2, sum_out, sum_in, qown, qpart, qt, m_s, l_s, acc, sc_a, sc_b, mean_s, dev_s,
    osend, orecv, ssend, srecv,
    loc_sem, w_sem, ring_ss, ring_rs, d2d_ss, d2d_rs, tok_ss, tok_rs, att_ss, att_rs,
    q_ss, q_rs, o_ss, o_rs, st_ss, st_rs, wo_ss, wo_rs, w2_ss, w2_rs, wx_ss, wx_rs, sum_ss, sum_rs,
):
    p, t = lax.axis_index("patch"), lax.axis_index("tensor")
    b, z, c = lax.div(p, 16), lax.rem(lax.div(p, 2), NZ), lax.rem(p, 2)
    yh, x = lax.div(t, 4), lax.rem(t, 4)

    def dev(b=b, z=z, c=c, yh=yh, x=x):
        return (b * 16 + z * 2 + c, yh * 4 + x)

    def remote(src, dst, ss, rs, to):
        return pltpu.make_async_remote_copy(
            src_ref=src, dst_ref=dst, send_sem=ss, recv_sem=rs, device_id=to, device_id_type=MESH
        )

    dz = (1 - 2 * c, 2 * c - 1)
    zs = tuple(lax.rem(z + s + NZ, NZ) for s in dz)
    sibling, partner = dev(c=1 - c), dev(b=1 - b)
    xr, xl = dev(x=lax.rem(x + 1, 4)), dev(x=lax.rem(x + 3, 4))
    yo = dev(yh=1 - yh)
    me = z * 2 + c

    tok_load = pltpu.make_async_copy(tok_in, tok.at[t], loc_sem.at[0])
    k_loads, v_loads = [], []
    for h in range(NH):
        cols = pl.ds(h * HD, HD)
        k_loads.append(pltpu.make_async_copy(sk_in.at[:, cols], kv.at[me, h, 0], loc_sem.at[1 + 2 * h]))
        v_loads.append(pltpu.make_async_copy(sv_in.at[:, cols], vtmp.at[h], loc_sem.at[2 + 2 * h]))
    w_loads = [pltpu.make_async_copy(w_in.at[j], w.at[j], w_sem.at[j]) for j in range(3)]
    for copy in v_loads + k_loads + [tok_load] + w_loads:
        copy.start()

    barrier = pltpu.get_barrier_semaphore()
    peers = [sibling, partner, dev(z=zs[0]), dev(z=zs[1])]
    for e in range(1, NT):
        peers.append((p, lax.rem(t + e, NT)))
    for peer in peers:
        pl.semaphore_signal(barrier, inc=1, device_id=peer, device_id_type=MESH)

    def put_values(slot, h, values):
        kv[slot, h, 1, :HD] = values[:HD].T
        kv[slot, h, 1, HD:] = values[HD:].T

    for h in range(NH):
        v_loads[h].wait()
        put_values(me, h, vtmp[h])
    for copy in k_loads + [tok_load]:
        copy.wait()
    pl.semaphore_wait(barrier, len(peers))

    sent = []

    def go(make, *args):
        make(*args).start()
        sent.append((make, args))

    def drain():
        for make, args in sent:
            make(*args).wait_send()
        sent.clear()

    def slot_of(s, d):
        return lax.rem(z - d * dz[s] + NZ, NZ) * 2 + c

    def unit(slot, u):
        return kv.at[slot, u // 2, u % 2]

    def ring(s, u, d):
        view = unit(slot_of(s, d), u)
        return remote(view, view, ring_ss.at[s, u, d], ring_rs.at[s, u, d], dev(z=zs[s]))

    def share(k, u, slot):
        return remote(unit(slot, u), unit(slot, u), d2d_ss.at[k, u], d2d_rs.at[k, u], sibling)

    def own(u):
        go(ring, 0, u, 0)
        go(ring, 1, u, 0)
        go(share, 0, u, me)

    def event(u, d):
        for s in (0, 1):
            if d > DEPTH[s]:
                continue
            slot = slot_of(s, d)
            remote(
                unit(slot, u), unit(slot, u), ring_ss.at[s, u, d - 1], ring_rs.at[s, u, d - 1], sibling
            ).wait_recv()
            if d < DEPTH[s]:
                go(ring, s, u, d)
            go(share, d + 4 * s, u, slot)

    slot_l, slot_r, slot_f = (yh * 4 + lax.rem(x + e, 4) for e in (3, 1, 2))
    slot_y, slot_yl, slot_yr, slot_yf = ((1 - yh) * 4 + lax.rem(x + e, 4) for e in (0, 3, 1, 2))
    rows = (pl.ds(0, ROWS // 2), pl.ds(ROWS // 2, ROWS // 2))

    def tok_copy(slot, half, to, i):
        view = tok.at[slot, rows[half]]
        return remote(view, view, tok_ss.at[i], tok_rs.at[i], to)

    def tok_wait(slot, half, i):
        tok_copy(slot, half, sibling, i).wait_recv()

    def wo_cols(to):
        return pl.ds(pl.multiple_of(to * WIDTH, WIDTH), WIDTH)

    def wo_near(e, g):
        to = lax.rem(x + e, 4)
        src = wo_in.at[pl.ds(0, 2), c, :, wo_cols(g * 4 + to)]
        return remote(src, wo.at[x, g, :, c], wo_ss.at[2 * e + g], wo_rs.at[2 * e + g], dev(x=to))

    def wo_near_own(g):
        src = wo_in.at[pl.ds(0, 2), c, :, wo_cols(g * 4 + x)]
        return pltpu.make_async_copy(src, wo.at[x, g, :, c], wo_ss.at[g])

    def wo_all(e):
        to = yh * 4 + lax.rem(x + e, 4) if e < 4 else (1 - yh) * 4 + lax.rem(x + e, 4)
        src = wo_in.at[2, c, :, wo_cols(to)]
        return remote(src, wo2.at[t, c], w2_ss.at[e], w2_rs.at[e], (p, to))

    def wo_all_own():
        return pltpu.make_async_copy(wo_in.at[2, c, :, wo_cols(t)], wo2.at[t, c], w2_ss.at[0])

    def wo_share(half):
        return remote(wo.at[:, :, :, half], wo.at[:, :, :, half], wx_ss.at[0], wx_rs.at[0], sibling)

    def wo_share2(half):
        return remote(wo2.at[:, half], wo2.at[:, half], wx_ss.at[1], wx_rs.at[1], sibling)

    def wo_pass():
        for e in range(1, 4):
            for g in (0, 1):
                view = wo.at[lax.rem(x + 4 - e, 4), g, :, c]
                remote(view, view, wo_ss.at[2 * e + g], wo_rs.at[2 * e + g], sibling).wait_recv()
        for g in (0, 1):
            wo_near_own(g).wait()
        go(wo_share, c)

    def wo_pass2():
        for e in range(1, NT):
            frm = yh * 4 + lax.rem(x + 4 - e, 4) if e < 4 else (1 - yh) * 4 + lax.rem(x + 8 - e, 4)
            view = wo2.at[frm, c]
            remote(view, view, w2_ss.at[e], w2_rs.at[e], sibling).wait_recv()
        wo_all_own().wait()
        go(wo_share2, c)

    def stats(slot, seen):
        xb = tok[slot].astype(F32)
        mb = jnp.sum(xb, axis=1, keepdims=True) * (1.0 / WIDTH)
        cb = xb - mb
        sb = jnp.sum(cb * cb, axis=1, keepdims=True)
        if seen == 0:
            mean_s[...] = mb
            dev_s[...] = sb
        else:
            delta = mb - mean_s[...]
            mean_s[...] += delta * (1.0 / (seen + 1))
            dev_s[...] += sb + delta * delta * (WIDTH * seen / (seen + 1))

    def place(n):
        h, i = n // 8, n % 8
        d, side = (i + 1) // 2, (i + 1) % 2
        chip = lax.rem(z - d * dz[side] + NZ, NZ)
        if d in (0, 4):
            k = d
        else:
            k = d if side else d + 4
        return h, i, k, chip * 2 + c, chip * 2 + 1 - c

    def block_wait(n, j):
        h, _, k, _, far = place(n)
        share(k, 2 * h + j, far).wait_recv()

    def scores(n):
        h, i, _, near, far = place(n)
        buf = (sc_a, sc_b)[n % 2]
        query = qt[h]
        if i == 0:
            first = jnp.concatenate(
                [dot(kv[FRESH, h, 0], query[:, :ROWS]), dot(kv[near, h, 0], query[:, ROWS:])], axis=1
            )
        else:
            first = dot(kv[near, h, 0], query)
        top = None
        for j, s in enumerate((first, dot(kv[far, h, 0], query))):
            s = s * EXP_SCALE
            buf[j] = s
            part = s.max(axis=0, keepdims=True)
            top = part if top is None else jnp.maximum(top, part)
        return top

    def values(slot, h):
        return jnp.concatenate([kv[slot, h, 1, :HD], kv[slot, h, 1, HD:]], axis=1)

    def weigh(n, top):
        h, i, _, near, far = place(n)
        buf = (sc_a, sc_b)[n % 2]
        new = top if i == 0 else jnp.maximum(m_s[h], top)
        total, summed = None, None
        for j, slot in enumerate((near, far)):
            weights = jnp.exp2(buf[j] - new)
            part = jnp.sum(weights, axis=0, keepdims=True)
            weights = weights.astype(BF16)
            if i == 0 and j == 0:
                prod = jnp.concatenate(
                    [dot(values(FRESH, h), weights[:, :ROWS]), dot(values(slot, h), weights[:, ROWS:])], axis=1
                )
            else:
                prod = dot(values(slot, h), weights)
            total = part if total is None else total + part
            summed = prod if summed is None else summed + prod
        if i == 0:
            l_s[h] = total
            acc[h] = summed
        else:
            alpha = jnp.exp2(m_s[h] - new)
            l_s[h] = l_s[h] * alpha + total
            acc[h] = acc[h] * alpha + summed
        m_s[h] = new

    def o_copy(h):
        return remote(osend.at[h], orecv.at[h], o_ss.at[h], o_rs.at[h], partner)

    def s_copy(h):
        return remote(ssend.at[h], srecv.at[h], st_ss.at[h], st_rs.at[h], partner)

    def q_copy(h):
        return remote(qown.at[h], qpart.at[h], q_ss.at[h], q_rs.at[h], partner)

    def give(h):
        total = l_s[h, :, ROWS:]
        osend[h] = (acc[h, :, ROWS:] / total).astype(BF16)
        ssend[h, 0:1, :] = m_s[h, :, ROWS:]
        ssend[h, 1:2, :] = total
        go(o_copy, h)
        go(s_copy, h)

    def att_copy(h, e):
        if h < 2:
            view, to = att.at[h, x], dev(x=lax.rem(x + e, 4))
        else:
            view, to = att2.at[t], (p, lax.rem(t + e, NT))
        return remote(view, view, att_ss.at[h, e], att_rs.at[h, e], to)

    def att_wait(h):
        for e in range(1, 4 if h < 2 else NT):
            view = att.at[h, lax.rem(x + 4 - e, 4)] if h < 2 else att2.at[lax.rem(t + NT - e, NT)]
            remote(view, view, att_ss.at[h, e], att_rs.at[h, e], sibling).wait_recv()

    def merge(h):
        o_copy(h).wait_recv()
        s_copy(h).wait_recv()
        m1, m2 = m_s[h, :, :ROWS], srecv[h, 0:1, :]
        top = jnp.maximum(m1, m2)
        w1 = jnp.exp2(m1 - top)
        w2 = jnp.exp2(m2 - top) * srecv[h, 1:2, :]
        inv = 1.0 / (l_s[h, :, :ROWS] * w1 + w2)
        attended = acc[h, :, :ROWS] * (w1 * inv) + orecv[h].astype(F32) * (w2 * inv)
        attended = attended.T.astype(BF16)
        if h < 2:
            att[h, x] = attended
        else:
            att2[t] = attended
        for e in range(1, 4 if h < 2 else NT):
            go(att_copy, h, e)

    def project(g):
        total = None
        for s in range(4):
            lhs = jnp.concatenate([att[0, s], att[1, s]], axis=1)
            part = dot(lhs, wo[s, g].reshape(2 * HD, WIDTH))
            total = part if total is None else total + part
        return total

    def project_last():
        total = None
        for s in range(0, NT, 2):
            lhs = jnp.concatenate([att2[s], att2[s + 1]], axis=1)
            part = dot(lhs, wo2[pl.ds(s, 2)].reshape(2 * HD, WIDTH))
            total = part if total is None else total + part
        return total

    def sum_copy():
        return remote(sum_out, sum_in, sum_ss.at[0], sum_rs.at[0], yo)

    for u in range(5):
        own(u)
    for i in (0, 1):
        go(tok_copy, t, i, yo, 4 + i)
        go(tok_copy, t, i, xr, 0 + i)
        go(tok_copy, t, i, xl, 2 + i)
    stats(t, 0)
    tok_wait(slot_l, 0, 0)
    go(tok_copy, slot_l, 0, xr, 6)
    tok_wait(slot_y, 0, 4)
    go(tok_copy, slot_y, 0, xr, 8)
    go(tok_copy, slot_y, 0, xl, 10)
    tok_wait(slot_r, 1, 3)
    go(tok_copy, slot_r, 1, xl, 7)
    tok_wait(slot_y, 1, 5)
    go(tok_copy, slot_y, 1, xr, 9)
    go(tok_copy, slot_y, 1, xl, 11)
    event(0, 1)
    event(1, 1)
    event(2, 1)
    own(5)
    tok_wait(slot_l, 1, 1)
    tok_wait(slot_r, 0, 2)
    stats(slot_l, 1)
    stats(slot_r, 2)
    tok_wait(slot_f, 0, 6)
    go(tok_copy, slot_f, 0, yo, 12)
    tok_wait(slot_f, 1, 7)
    go(tok_copy, slot_f, 1, yo, 13)
    stats(slot_y, 3)
    stats(slot_f, 4)
    event(0, 2)
    event(1, 2)
    event(3, 1)
    for i in (0, 1):
        tok_wait(slot_yl, i, 8 + i)
        tok_wait(slot_yr, i, 10 + i)
    stats(slot_yl, 5)
    stats(slot_yr, 6)
    event(2, 2)
    tok_wait(slot_yf, 0, 12)
    tok_wait(slot_yf, 1, 13)
    stats(slot_yf, 7)
    for g in (0, 1):
        wo_near_own(g).start()
        for e in (1, 2, 3):
            go(wo_near, e, g)
    wo_all_own().start()
    for e in (1, 2, 3):
        go(wo_all, e)
    mean = mean_s[...]
    inv = lax.rsqrt(dev_s[...] * (1.0 / D) + 1e-6)
    for i in range(NT):
        cols = slice(i * WIDTH, (i + 1) * WIDTH)
        normed = (tok[i].astype(F32) - mean) * inv
        mod[:, cols] = (normed * (1.0 + scale_ref[:, cols]) + shift_ref[:, cols]).astype(BF16)
    after = {0: [(0, 3), (1, 3)], 1: [(4, 1), (3, 2)], 2: [(5, 1), (2, 3)]}
    for j in range(3):
        w_loads[j].wait()
        res = dot(mod[...], w[j]).astype(BF16)
        for h in range(NH):
            head = res[:, h * HD : (h + 1) * HD]
            if j == 0:
                qown[h] = head
                go(q_copy, h)
                qt[h, :, :ROWS] = head.T
            elif j == 1:
                kv[FRESH, h, 0] = head
            else:
                put_values(FRESH, h, head)
        for u, d in after[j]:
            event(u, d)
    for h in range(NH):
        q_copy(h).wait_recv()
        qt[h, :, ROWS:] = qpart[h].T
    for e in (4, 5, 6, 7):
        go(wo_all, e)

    before = {
        1: [(0, 4), (1, 4)],
        3: [(4, 2), (3, 3)],
        6: [(5, 2), (2, 4)],
        9: [(4, 3)],
        11: [(3, 4)],
        13: [(5, 3)],
        20: [(4, 4)],
        21: [(5, 4)],
    }
    extra = {
        8: lambda: give(0),
        15: lambda: merge(0),
        16: lambda: give(1),
        18: wo_pass,
        19: wo_pass2,
        21: lambda: merge(1),
    }
    block_wait(0, 0)
    top = scores(0)
    for n in range(8 * NH):
        for u, d in before.get(n, ()):
            event(u, d)
        if n in extra:
            extra[n]()
        block_wait(n, 1)
        if n + 1 < 8 * NH:
            block_wait(n + 1, 0)
            later = scores(n + 1)
        weigh(n, top)
        top = later
    give(2)
    att_wait(0)
    att_wait(1)
    wo_share(1 - c).wait_recv()
    sum_out[...] = project(1 - yh).astype(BF16)
    go(sum_copy)
    out_ref[...] = project(yh)
    merge(2)
    wo_share2(1 - c).wait_recv()
    sum_copy().wait_recv()
    out_ref[...] += sum_in[...].astype(F32)
    drain()
    att_wait(2)
    out_ref[...] += project_last()


def block(tokens, scale, shift, w, wo, sk, sv):
    dma, vmem = pltpu.SemaphoreType.DMA, pltpu.VMEM
    anywhere = pl.BlockSpec(memory_space=pl.ANY)
    inside = pl.BlockSpec(memory_space=pltpu.VMEM)
    return pl.pallas_call(
        kernel,
        out_shape=jax.ShapeDtypeStruct((ROWS, WIDTH), F32),
        in_specs=[anywhere, inside, inside, anywhere, anywhere, anywhere, anywhere],
        out_specs=inside,
        scratch_shapes=[
            vmem((2 * NZ + 1, NH, 2, ROWS, HD), BF16),
            vmem((NH, ROWS, HD), BF16),
            vmem((NT, ROWS, WIDTH), BF16),
            vmem((ROWS, D), BF16),
            vmem((3, D, WIDTH), BF16),
            vmem((4, 2, 2, 2, 64, WIDTH), BF16),
            vmem((NT, 2, 64, WIDTH), BF16),
            vmem((2, 4, ROWS, HD), BF16),
            vmem((NT, ROWS, HD), BF16),
            vmem((ROWS, WIDTH), BF16),
            vmem((ROWS, WIDTH), BF16),
            vmem((NH, ROWS, HD), BF16),
            vmem((NH, ROWS, HD), BF16),
            vmem((NH, HD, 2 * ROWS), BF16),
            vmem((NH, 1, 2 * ROWS), F32),
            vmem((NH, 1, 2 * ROWS), F32),
            vmem((NH, HD, 2 * ROWS), F32),
            vmem((2, ROWS, 2 * ROWS), F32),
            vmem((2, ROWS, 2 * ROWS), F32),
            vmem((ROWS, 1), F32),
            vmem((ROWS, 1), F32),
            vmem((NH, HD, ROWS), BF16),
            vmem((NH, HD, ROWS), BF16),
            vmem((NH, 8, ROWS), F32),
            vmem((NH, 8, ROWS), F32),
            dma((8,)),
            dma((3,)),
            dma((2, 2 * NH, 4)),
            dma((2, 2 * NH, 4)),
            dma((8, 2 * NH)),
            dma((8, 2 * NH)),
            dma((14,)),
            dma((14,)),
            dma((NH, NT)),
            dma((NH, NT)),
            dma((NH,)),
            dma((NH,)),
            dma((NH,)),
            dma((NH,)),
            dma((NH,)),
            dma((NH,)),
            dma((NT,)),
            dma((NT,)),
            dma((NT,)),
            dma((NT,)),
            dma((2,)),
            dma((2,)),
            dma((1,)),
            dma((1,)),
        ],
        compiler_params=pltpu.CompilerParams(
            collective_id=0, has_side_effects=True, vmem_limit_bytes=56 * 1024 * 1024
        ),
        name="attention_block",
    )(tokens, scale, shift, w, wo, sk, sv)


def local(tokens, shift, scale, gate, w_qkv, w_out, stale_keys, stale_values):
    summed = block(
        tokens,
        scale.reshape(1, D),
        shift.reshape(1, D),
        jnp.transpose(w_qkv, (1, 0, 2)),
        w_out.reshape(NH, 2, 64, D),
        stale_keys,
        stale_values,
    )
    branch = gate * summed
    return ((tokens.astype(F32) + branch).astype(BF16), branch)


def solution(mesh):
    in_specs = (
        P("patch", "tensor"),
        P(),
        P(),
        P("tensor"),
        P(None, None, "tensor"),
        P("tensor", None),
        P("patch", "tensor"),
        P("patch", "tensor"),
    )
    out_specs = (P("patch", "tensor"), P("patch", "tensor"))
    return jax.shard_map(local, mesh=mesh, in_specs=in_specs, out_specs=out_specs, check_vma=False)
```

time: 95.7 us -> 69.5 us (0.73); the launches traced: 95.5 us -> 68.3 us
  Pallas kernels: 93 us -> 65.7 us
    pallas_call x1, Pallas kernels: 93 us -> 65.7 us  [block(): pl.pallas_call(kernel, out_shape=jax.ShapeDtypeStruct((ROWS, WIDTH), F32)...]
where the time goes in v2:
time: 69.5 us; the launch traced here: 68.3 us
  Pallas kernels  65.7 us (95%)
  other arithmetic  1.85 us (3%)
    pallas_call x1, Pallas kernels, block(): pl.pallas_call(kernel, out_shape=jax.ShapeDtypeStruct((ROWS, WIDTH), F32)...  65.7 us
    convert_element_type x1, other arithmetic, local(): return ((tokens.astype(F32) + branch).astype(BF16), branch)  1.85 us

profile of v2, /device:TPU:2, one launch (start us, length us, event | category | flops | bytes accessed | tf_op | source)
XLA Modules:
  0.0 68.3 jit_solution(8106634366190522825)
XLA Ops:
  0.6 0.0 copy-start
  0.6 0.0 copy-start.1
  0.7 65.7 %attention_block.1 = f32[256,384]{1,0:T(8,128)} custom-call(bf16[256,384]{1,0:T(8,128)(2,1)} %tok_in.1, f32[1,3072]{1,0:T(1,128)} %bitcast.6, f32[1,3072]{1,0:T(1,128)} %bitcast.7, bf16[3,3072,384]{2,1,0:T(8,128)(2,1)} %bitcast.4, bf16[3,2,64,3072]{3,2,1,0:T(8,128)(2,1)} %bitcast.5, bf16[256,384]{1,0:T(8,128)(2,1)} %sk_in.1, bf16[256,384]{1,0:T(8,128)(2,1)} %sv_in.1), custom_call_target="tpu_custom_call" | custom-call | tf_op jit(solution)/shard_map/attention_block/pallas_call | solution.py:446
  66.4 0.0 copy-done
  66.4 0.0 copy-done.1
  66.4 1.9 %add_convert_fusion = (bf16[256,384]{1,0:T(8,128)(2,1)}, f32[256,384]{1,0:T(8,128)}) fusion(bf16[256,384]{1,0:T(8,128)(2,1)S(1)} %copy-done, f32[256,384]{1,0:T(8,128)} %attention_block.1, f32[384]{0:T(512)S(1)} %copy-done.1), kind=kLoop, calls=%fused_computation | loop fusion | flops 393216 | bytes 1181184 | tf_op jit(solution)/shard_map/convert_element_type | solution.py:520
Async XLA Ops:
  0.6 65.8 %copy-start = (bf16[256,384]{1,0:T(8,128)(2,1)S(1)}, bf16[256,384]{1,0:T(8,128)(2,1)}, u32[]{:S(2)}) copy-start(bf16[256,384]{1,0:T(8,128)(2,1)} %tok_in.1) | copy-start | bytes 589828
  0.6 65.8 %copy-start.1 = (f32[384]{0:T(512)S(1)}, f32[384]{0:T(512)}, u32[]{:S(2)}) copy-start(f32[384]{0:T(512)} %param.11) | copy-start | bytes 4612

commit v3 on v2

--- a/solution.py
+++ b/solution.py
@@ -26,9 +26,9 @@
 
 
 def kernel(
-    tok_in, scale_ref, shift_ref, w_in, wo_in, sk_in, sv_in,
+    tok_in, scale_in, shift_in, w_in, wo_in, sk_in, sv_in,
     out_ref,
-    kv, vtmp, tok, mod, w, wo, wo2, att, att2, sum_out, sum_in, qown, qpart, qt, m_s, l_s, acc, sc_a, sc_b, mean_s, dev_s,
+    scale_ref, shift_ref, kv, vtmp, tok, mod, w, wo, wo2, att, att2, sum_out, sum_in, qown, qpart, qt, m_s, l_s, acc, sc_a, sc_b, mean_s, dev_s,
     osend, orecv, ssend, srecv,
     loc_sem, w_sem, ring_ss, ring_rs, d2d_ss, d2d_rs, tok_ss, tok_rs, att_ss, att_rs,
     q_ss, q_rs, o_ss, o_rs, st_ss, st_rs, wo_ss, wo_rs, w2_ss, w2_rs, wx_ss, wx_rs, sum_ss, sum_rs,
@@ -52,22 +52,26 @@
     yo = dev(yh=1 - yh)
     me = z * 2 + c
 
+    barrier = pltpu.get_barrier_semaphore()
+    peers = [sibling, partner, dev(z=zs[0]), dev(z=zs[1])]
+    for e in range(1, NT):
+        peers.append((p, lax.rem(t + e, NT)))
+    for peer in peers:
+        pl.semaphore_signal(barrier, inc=1, device_id=peer, device_id_type=MESH)
+
     tok_load = pltpu.make_async_copy(tok_in, tok.at[t], loc_sem.at[0])
     k_loads, v_loads = [], []
     for h in range(NH):
         cols = pl.ds(h * HD, HD)
         k_loads.append(pltpu.make_async_copy(sk_in.at[:, cols], kv.at[me, h, 0], loc_sem.at[1 + 2 * h]))
         v_loads.append(pltpu.make_async_copy(sv_in.at[:, cols], vtmp.at[h], loc_sem.at[2 + 2 * h]))
+    vec_loads = [
+        pltpu.make_async_copy(scale_in, scale_ref, loc_sem.at[7]),
+        pltpu.make_async_copy(shift_in, shift_ref, loc_sem.at[8]),
+    ]
     w_loads = [pltpu.make_async_copy(w_in.at[j], w.at[j], w_sem.at[j]) for j in range(3)]
-    for copy in v_loads + k_loads + [tok_load] + w_loads:
+    for copy in v_loads + k_loads + [tok_load] + vec_loads + w_loads:
         copy.start()
-
-    barrier = pltpu.get_barrier_semaphore()
-    peers = [sibling, partner, dev(z=zs[0]), dev(z=zs[1])]
-    for e in range(1, NT):
-        peers.append((p, lax.rem(t + e, NT)))
-    for peer in peers:
-        pl.semaphore_signal(barrier, inc=1, device_id=peer, device_id_type=MESH)
 
     def put_values(slot, h, values):
         kv[slot, h, 1, :HD] = values[:HD].T
@@ -188,34 +192,35 @@
             mean_s[...] += delta * (1.0 / (seen + 1))
             dev_s[...] += sb + delta * delta * (WIDTH * seen / (seen + 1))
 
-    def place(n):
-        h, i = n // 8, n % 8
+    def place(h, i):
         d, side = (i + 1) // 2, (i + 1) % 2
         chip = lax.rem(z - d * dz[side] + NZ, NZ)
         if d in (0, 4):
             k = d
         else:
             k = d if side else d + 4
-        return h, i, k, chip * 2 + c, chip * 2 + 1 - c
-
-    def block_wait(n, j):
-        h, _, k, _, far = place(n)
+        return k, chip * 2 + c, chip * 2 + 1 - c
+
+    def block_wait(h, i, j):
+        k, _, far = place(h, i)
         share(k, 2 * h + j, far).wait_recv()
 
-    def scores(n):
-        h, i, _, near, far = place(n)
-        buf = (sc_a, sc_b)[n % 2]
-        query = qt[h]
+    def scores(h, i, lo, hi, buf):
+        _, near, far = place(h, i)
+        query = qt[h, :, lo:hi]
         if i == 0:
-            first = jnp.concatenate(
-                [dot(kv[FRESH, h, 0], query[:, :ROWS]), dot(kv[near, h, 0], query[:, ROWS:])], axis=1
-            )
+            parts = []
+            if lo == 0:
+                parts.append(dot(kv[FRESH, h, 0], query[:, :ROWS]))
+            if hi > ROWS:
+                parts.append(dot(kv[near, h, 0], query[:, ROWS - lo :]))
+            first = parts[0] if len(parts) == 1 else jnp.concatenate(parts, axis=1)
         else:
             first = dot(kv[near, h, 0], query)
         top = None
         for j, s in enumerate((first, dot(kv[far, h, 0], query))):
             s = s * EXP_SCALE
-            buf[j] = s
+            buf[j, :, lo:hi] = s
             part = s.max(axis=0, keepdims=True)
             top = part if top is None else jnp.maximum(top, part)
         return top
@@ -223,31 +228,33 @@
     def values(slot, h):
         return jnp.concatenate([kv[slot, h, 1, :HD], kv[slot, h, 1, HD:]], axis=1)
 
-    def weigh(n, top):
-        h, i, _, near, far = place(n)
-        buf = (sc_a, sc_b)[n % 2]
-        new = top if i == 0 else jnp.maximum(m_s[h], top)
+    def weigh(h, i, lo, hi, buf, top):
+        _, near, far = place(h, i)
+        new = top if i == 0 else jnp.maximum(m_s[h, :, lo:hi], top)
         total, summed = None, None
         for j, slot in enumerate((near, far)):
-            weights = jnp.exp2(buf[j] - new)
+            weights = jnp.exp2(buf[j, :, lo:hi] - new)
             part = jnp.sum(weights, axis=0, keepdims=True)
             weights = weights.astype(BF16)
             if i == 0 and j == 0:
-                prod = jnp.concatenate(
-                    [dot(values(FRESH, h), weights[:, :ROWS]), dot(values(slot, h), weights[:, ROWS:])], axis=1
-                )
+                parts = []
+                if lo == 0:
+                    parts.append(dot(values(FRESH, h), weights[:, :ROWS]))
+                if hi > ROWS:
+                    parts.append(dot(values(slot, h), weights[:, ROWS - lo :]))
+                prod = parts[0] if len(parts) == 1 else jnp.concatenate(parts, axis=1)
             else:
                 prod = dot(values(slot, h), weights)
             total = part if total is None else total + part
             summed = prod if summed is None else summed + prod
         if i == 0:
-            l_s[h] = total
-            acc[h] = summed
-        else:
-            alpha = jnp.exp2(m_s[h] - new)
-            l_s[h] = l_s[h] * alpha + total
-            acc[h] = acc[h] * alpha + summed
-        m_s[h] = new
+            l_s[h, :, lo:hi] = total
+            acc[h, :, lo:hi] = summed
+        else:
+            alpha = jnp.exp2(m_s[h, :, lo:hi] - new)
+            l_s[h, :, lo:hi] = l_s[h, :, lo:hi] * alpha + total
+            acc[h, :, lo:hi] = acc[h, :, lo:hi] * alpha + summed
+        m_s[h, :, lo:hi] = new
 
     def o_copy(h):
         return remote(osend.at[h], orecv.at[h], o_ss.at[h], o_rs.at[h], partner)
@@ -270,13 +277,22 @@
         if h < 2:
             view, to = att.at[h, x], dev(x=lax.rem(x + e, 4))
         else:
-            view, to = att2.at[t], (p, lax.rem(t + e, NT))
+            view = att2.at[t]
+            to = yo if e == 4 else dev(x=lax.rem(x + e, 4))
         return remote(view, view, att_ss.at[h, e], att_rs.at[h, e], to)
 
-    def att_wait(h):
-        for e in range(1, 4 if h < 2 else NT):
-            view = att.at[h, lax.rem(x + 4 - e, 4)] if h < 2 else att2.at[lax.rem(t + NT - e, NT)]
-            remote(view, view, att_ss.at[h, e], att_rs.at[h, e], sibling).wait_recv()
+    def att_pass(e):
+        view = att2.at[slot_y]
+        return remote(view, view, att_ss.at[2, 4 + e], att_rs.at[2, 4 + e], dev(x=lax.rem(x + e, 4)))
+
+    def att_wait(h, e):
+        if h < 2:
+            view = att.at[h, lax.rem(x + 4 - e, 4)]
+        elif e < 4:
+            view = att2.at[yh * 4 + lax.rem(x + 4 - e, 4)]
+        else:
+            view = att2.at[(1 - yh) * 4 + lax.rem(x + 8 - e, 4)]
+        remote(view, view, att_ss.at[h, e], att_rs.at[h, e], sibling).wait_recv()
 
     def merge(h):
         o_copy(h).wait_recv()
@@ -292,7 +308,7 @@
             att[h, x] = attended
         else:
             att2[t] = attended
-        for e in range(1, 4 if h < 2 else NT):
+        for e in (1, 3, 2) if h < 2 else (4, 1, 3, 2):
             go(att_copy, h, e)
 
     def project(g):
@@ -314,40 +330,41 @@
     def sum_copy():
         return remote(sum_out, sum_in, sum_ss.at[0], sum_rs.at[0], yo)
 
-    for u in range(5):
-        own(u)
     for i in (0, 1):
         go(tok_copy, t, i, yo, 4 + i)
         go(tok_copy, t, i, xr, 0 + i)
         go(tok_copy, t, i, xl, 2 + i)
+    for u in range(4):
+        own(u)
     stats(t, 0)
     tok_wait(slot_l, 0, 0)
     go(tok_copy, slot_l, 0, xr, 6)
     tok_wait(slot_y, 0, 4)
     go(tok_copy, slot_y, 0, xr, 8)
     go(tok_copy, slot_y, 0, xl, 10)
+    event(0, 1)
     tok_wait(slot_r, 1, 3)
     go(tok_copy, slot_r, 1, xl, 7)
     tok_wait(slot_y, 1, 5)
     go(tok_copy, slot_y, 1, xr, 9)
     go(tok_copy, slot_y, 1, xl, 11)
-    event(0, 1)
     event(1, 1)
     event(2, 1)
-    own(5)
     tok_wait(slot_l, 1, 1)
     tok_wait(slot_r, 0, 2)
-    stats(slot_l, 1)
-    stats(slot_r, 2)
     tok_wait(slot_f, 0, 6)
     go(tok_copy, slot_f, 0, yo, 12)
     tok_wait(slot_f, 1, 7)
     go(tok_copy, slot_f, 1, yo, 13)
+    event(3, 1)
+    own(4)
+    own(5)
+    stats(slot_l, 1)
+    stats(slot_r, 2)
     stats(slot_y, 3)
     stats(slot_f, 4)
     event(0, 2)
     event(1, 2)
-    event(3, 1)
     for i in (0, 1):
         tok_wait(slot_yl, i, 8 + i)
         tok_wait(slot_yr, i, 10 + i)
@@ -364,16 +381,25 @@
     wo_all_own().start()
     for e in (1, 2, 3):
         go(wo_all, e)
+    for copy in vec_loads:
+        copy.wait()
     mean = mean_s[...]
     inv = lax.rsqrt(dev_s[...] * (1.0 / D) + 1e-6)
-    for i in range(NT):
-        cols = slice(i * WIDTH, (i + 1) * WIDTH)
-        normed = (tok[i].astype(F32) - mean) * inv
-        mod[:, cols] = (normed * (1.0 + scale_ref[:, cols]) + shift_ref[:, cols]).astype(BF16)
-    after = {0: [(0, 3), (1, 3)], 1: [(4, 1), (3, 2)], 2: [(5, 1), (2, 3)]}
+    after = {0: [(3, 2)], 1: [(4, 1)], 2: [(5, 1)]}
     for j in range(3):
         w_loads[j].wait()
-        res = dot(mod[...], w[j]).astype(BF16)
+        if j == 0:
+            res = None
+            for i in range(NT):
+                cols = slice(i * WIDTH, (i + 1) * WIDTH)
+                normed = (tok[i].astype(F32) - mean) * inv
+                slab = (normed * (1.0 + scale_ref[:, cols]) + shift_ref[:, cols]).astype(BF16)
+                mod[:, cols] = slab
+                part = dot(slab, w[0, cols])
+                res = part if res is None else res + part
+        else:
+            res = dot(mod[...], w[j])
+        res = res.astype(BF16)
         for h in range(NH):
             head = res[:, h * HD : (h + 1) * HD]
             if j == 0:
@@ -386,56 +412,83 @@
                 put_values(FRESH, h, head)
         for u, d in after[j]:
             event(u, d)
-    for h in range(NH):
+    for e in (4, 5, 6, 7):
+        go(wo_all, e)
+
+    def query_in(h):
         q_copy(h).wait_recv()
         qt[h, :, ROWS:] = qpart[h].T
-    for e in (4, 5, 6, 7):
-        go(wo_all, e)
-
-    before = {
-        1: [(0, 4), (1, 4)],
-        3: [(4, 2), (3, 3)],
-        6: [(5, 2), (2, 4)],
-        9: [(4, 3)],
-        11: [(3, 4)],
-        13: [(5, 3)],
-        20: [(4, 4)],
-        21: [(5, 4)],
+
+    order = [(0, i, 0, ROWS) for i in range(5)] + [(0, i, ROWS, 2 * ROWS) for i in range(5)]
+    rest = [(1, i) for i in range(5)] + [(2, 0), (2, 1), (2, 2)]
+    rest += [(0, 5), (0, 6), (1, 5), (1, 6), (0, 7), (1, 7)] + [(2, i) for i in range(3, 8)]
+    order += [(h, i, 0, 2 * ROWS) for h, i in rest]
+    due = {
+        (0, 0, 0): [lambda: event(0, 3)],
+        (0, 0, ROWS): [lambda: query_in(0), lambda: event(1, 3)],
+        (1, 0, 0): [lambda: query_in(1)],
+        (1, 1, 0): [lambda: event(2, 3)],
+        (1, 3, 0): [lambda: event(3, 3)],
+        (1, 4, 0): [lambda: event(4, 2)],
+        (2, 0, 0): [lambda: query_in(2)],
+        (2, 2, 0): [lambda: event(5, 2)],
+        (0, 6, 0): [lambda: event(0, 4)],
+        (1, 5, 0): [lambda: event(1, 4)],
+        (1, 6, 0): [lambda: event(2, 4)],
+        (0, 7, 0): [lambda: event(3, 4), lambda: event(4, 3)],
+        (2, 3, 0): [lambda: give(0), lambda: event(5, 3)],
+        (2, 4, 0): [lambda: give(1), wo_pass],
+        (2, 5, 0): [wo_pass2],
+        (2, 6, 0): [lambda: event(4, 4), lambda: merge(0)],
+        (2, 7, 0): [lambda: merge(1), lambda: event(5, 4)],
     }
-    extra = {
-        8: lambda: give(0),
-        15: lambda: merge(0),
-        16: lambda: give(1),
-        18: wo_pass,
-        19: wo_pass2,
-        21: lambda: merge(1),
-    }
-    block_wait(0, 0)
-    top = scores(0)
-    for n in range(8 * NH):
-        for u, d in before.get(n, ()):
-            event(u, d)
-        if n in extra:
-            extra[n]()
-        block_wait(n, 1)
-        if n + 1 < 8 * NH:
-            block_wait(n + 1, 0)
-            later = scores(n + 1)
-        weigh(n, top)
-        top = later
+    groups = [0, 5, 10, 12, 14, 16, 18, 20] + list(range(21, len(order) + 1))
+    bufs = (sc_a, sc_b)
+    waited = set()
+
+    def ready(n, j):
+        h, i, lo, _ = order[n]
+        if j == 0:
+            for f in due.get((h, i, lo), ()):
+                f()
+        if (h, i, j) not in waited:
+            waited.add((h, i, j))
+            block_wait(h, i, j)
+
+    fresh_start = (0, 5)
+    for start, stop in zip(groups, groups[1:]):
+        last = stop if stop in fresh_start or stop == len(order) else stop + 1
+        for n in range(start if start in fresh_start else start + 1, last):
+            ready(n, 0)
+        for n in range(start, stop):
+            ready(n, 1)
+        if start in fresh_start:
+            top = scores(*order[start], bufs[start % 2])
+        for n in range(start, stop):
+            if n + 1 < last:
+                later = scores(*order[n + 1], bufs[(n + 1) % 2])
+            weigh(*order[n], bufs[n % 2], top)
+            top = later
     give(2)
-    att_wait(0)
-    att_wait(1)
     wo_share(1 - c).wait_recv()
+    merge(2)
+    for h in (0, 1):
+        for e in (1, 2, 3):
+            att_wait(h, e)
     sum_out[...] = project(1 - yh).astype(BF16)
     go(sum_copy)
     out_ref[...] = project(yh)
-    merge(2)
+    att_wait(2, 4)
+    for e in (1, 3, 2):
+        go(att_pass, e)
+    for e in (1, 2, 3):
+        att_wait(2, e)
     wo_share2(1 - c).wait_recv()
     sum_copy().wait_recv()
     out_ref[...] += sum_in[...].astype(F32)
     drain()
-    att_wait(2)
+    for e in (5, 6, 7):
+        att_wait(2, e)
     out_ref[...] += project_last()
 
 
@@ -446,9 +499,11 @@
     return pl.pallas_call(
         kernel,
         out_shape=jax.ShapeDtypeStruct((ROWS, WIDTH), F32),
-        in_specs=[anywhere, inside, inside, anywhere, anywhere, anywhere, anywhere],
+        in_specs=[anywhere] * 7,
         out_specs=inside,
         scratch_shapes=[
+            vmem((1, D), F32),
+            vmem((1, D), F32),
             vmem((2 * NZ + 1, NH, 2, ROWS, HD), BF16),
             vmem((NH, ROWS, HD), BF16),
             vmem((NT, ROWS, WIDTH), BF16),
@@ -474,7 +529,7 @@
             vmem((NH, HD, ROWS), BF16),
             vmem((NH, 8, ROWS), F32),
             vmem((NH, 8, ROWS), F32),
-            dma((8,)),
+            dma((9,)),
             dma((3,)),
             dma((2, 2 * NH, 4)),
             dma((2, 2 * NH, 4)),

time: 69.5 us -> 65.6 us (0.944)
  Pallas kernels: 65.7 us -> 62.3 us
    pallas_call x1, Pallas kernels: 65.7 us -> 62.3 us  [block(): pl.pallas_call(kernel, out_shape=jax.ShapeDtypeStruct((ROWS, WIDTH), F32)...]
where the time goes in v3:
time: 65.6 us; the launch traced here: 64.8 us
  Pallas kernels  62.3 us (95%)
  other arithmetic  1.85 us (3%)
  between operations  0.67 us (1%)
    pallas_call x1, Pallas kernels, block(): pl.pallas_call(kernel, out_shape=jax.ShapeDtypeStruct((ROWS, WIDTH), F32)...  62.3 us
    convert_element_type x1, other arithmetic, local(): return ((tokens.astype(F32) + branch).astype(BF16), branch)  1.85 us

profile of v3, /device:TPU:2, one launch (start us, length us, event | category | flops | bytes accessed | tf_op | source)
XLA Modules:
  0.0 64.8 jit_solution(18393539751308679190)
XLA Ops:
  0.6 0.0 copy-start
  0.6 0.0 copy-start.1
  0.7 62.3 %attention_block.1 = f32[256,384]{1,0:T(8,128)} custom-call(bf16[256,384]{1,0:T(8,128)(2,1)} %tok_in.1, f32[1,3072]{1,0:T(1,128)} %bitcast.6, f32[1,3072]{1,0:T(1,128)} %bitcast.7, bf16[3,3072,384]{2,1,0:T(8,128)(2,1)} %bitcast.4, bf16[3,2,64,3072]{3,2,1,0:T(8,128)(2,1)} %bitcast.5, bf16[256,384]{1,0:T(8,128)(2,1)} %sk_in.1, bf16[256,384]{1,0:T(8,128)(2,1)} %sv_in.1), custom_call_target="tpu_custom_call" | custom-call | tf_op jit(solution)/shard_map/attention_block/pallas_call | solution.py:499
  63.0 0.0 copy-done
  63.0 0.0 copy-done.1
  63.0 1.9 %add_convert_fusion = (bf16[256,384]{1,0:T(8,128)(2,1)}, f32[256,384]{1,0:T(8,128)}) fusion(bf16[256,384]{1,0:T(8,128)(2,1)S(1)} %copy-done, f32[256,384]{1,0:T(8,128)} %attention_block.1, f32[384]{0:T(512)S(1)} %copy-done.1), kind=kLoop, calls=%fused_computation | loop fusion | flops 393216 | bytes 1181184 | tf_op jit(solution)/shard_map/convert_element_type | solution.py:575
Async XLA Ops:
  0.6 62.3 %copy-start = (bf16[256,384]{1,0:T(8,128)(2,1)S(1)}, bf16[256,384]{1,0:T(8,128)(2,1)}, u32[]{:S(2)}) copy-start(bf16[256,384]{1,0:T(8,128)(2,1)} %tok_in.1) | copy-start | bytes 589828
  0.6 62.3 %copy-start.1 = (f32[384]{0:T(512)S(1)}, f32[384]{0:T(512)}, u32[]{:S(2)}) copy-start(f32[384]{0:T(512)} %param.11) | copy-start | bytes 4612

commit v4 on v3

--- a/solution.py
+++ b/solution.py
@@ -70,18 +70,14 @@
         pltpu.make_async_copy(shift_in, shift_ref, loc_sem.at[8]),
     ]
     w_loads = [pltpu.make_async_copy(w_in.at[j], w.at[j], w_sem.at[j]) for j in range(3)]
-    for copy in v_loads + k_loads + [tok_load] + vec_loads + w_loads:
+    for copy in [tok_load] + k_loads + v_loads + vec_loads + w_loads:
         copy.start()
 
     def put_values(slot, h, values):
         kv[slot, h, 1, :HD] = values[:HD].T
         kv[slot, h, 1, HD:] = values[HD:].T
 
-    for h in range(NH):
-        v_loads[h].wait()
-        put_values(me, h, vtmp[h])
-    for copy in k_loads + [tok_load]:
-        copy.wait()
+    tok_load.wait()
     pl.semaphore_wait(barrier, len(peers))
 
     sent = []
@@ -109,6 +105,11 @@
         return remote(unit(slot, u), unit(slot, u), d2d_ss.at[k, u], d2d_rs.at[k, u], sibling)
 
     def own(u):
+        if u % 2 == 0:
+            k_loads[u // 2].wait()
+        else:
+            v_loads[u // 2].wait()
+            put_values(me, u // 2, vtmp[u // 2])
         go(ring, 0, u, 0)
         go(ring, 1, u, 0)
         go(share, 0, u, me)
@@ -127,14 +128,14 @@
 
     slot_l, slot_r, slot_f = (yh * 4 + lax.rem(x + e, 4) for e in (3, 1, 2))
     slot_y, slot_yl, slot_yr, slot_yf = ((1 - yh) * 4 + lax.rem(x + e, 4) for e in (0, 3, 1, 2))
-    rows = (pl.ds(0, ROWS // 2), pl.ds(ROWS // 2, ROWS // 2))
-
-    def tok_copy(slot, half, to, i):
-        view = tok.at[slot, rows[half]]
-        return remote(view, view, tok_ss.at[i], tok_rs.at[i], to)
-
-    def tok_wait(slot, half, i):
-        tok_copy(slot, half, sibling, i).wait_recv()
+    L, R, Y, F, YL, YR, YF = range(0, 28, 4)
+
+    def tok_copy(slot, q, to, kind):
+        view = tok.at[slot, pl.ds(q * (ROWS // 4), ROWS // 4)]
+        return remote(view, view, tok_ss.at[kind + q], tok_rs.at[kind + q], to)
+
+    def tok_wait(slot, q, kind):
+        tok_copy(slot, q, sibling, kind).wait_recv()
 
     def wo_cols(to):
         return pl.ds(pl.multiple_of(to * WIDTH, WIDTH), WIDTH)
@@ -273,26 +274,34 @@
         go(o_copy, h)
         go(s_copy, h)
 
+    half = (pl.ds(0, ROWS // 2), pl.ds(ROWS // 2, ROWS // 2))
+
     def att_copy(h, e):
         if h < 2:
             view, to = att.at[h, x], dev(x=lax.rem(x + e, 4))
         else:
-            view = att2.at[t]
-            to = yo if e == 4 else dev(x=lax.rem(x + e, 4))
+            view, to = att2.at[t], dev(x=lax.rem(x + e, 4))
         return remote(view, view, att_ss.at[h, e], att_rs.at[h, e], to)
 
-    def att_pass(e):
-        view = att2.at[slot_y]
-        return remote(view, view, att_ss.at[2, 4 + e], att_rs.at[2, 4 + e], dev(x=lax.rem(x + e, 4)))
+    def att_cross(r):
+        view = att2.at[t, half[r]]
+        return remote(view, view, att_ss.at[2, 4 + r], att_rs.at[2, 4 + r], yo)
+
+    def att_pass(r, e):
+        view, i = att2.at[slot_y, half[r]], 5 + 3 * r + e
+        return remote(view, view, att_ss.at[2, i], att_rs.at[2, i], dev(x=lax.rem(x + e, 4)))
 
     def att_wait(h, e):
-        if h < 2:
-            view = att.at[h, lax.rem(x + 4 - e, 4)]
-        elif e < 4:
-            view = att2.at[yh * 4 + lax.rem(x + 4 - e, 4)]
-        else:
-            view = att2.at[(1 - yh) * 4 + lax.rem(x + 8 - e, 4)]
+        view = att.at[h, lax.rem(x + 4 - e, 4)] if h < 2 else att2.at[yh * 4 + lax.rem(x + 4 - e, 4)]
         remote(view, view, att_ss.at[h, e], att_rs.at[h, e], sibling).wait_recv()
+
+    def att_wait_cross(r):
+        view = att2.at[slot_y, half[r]]
+        remote(view, view, att_ss.at[2, 4 + r], att_rs.at[2, 4 + r], sibling).wait_recv()
+
+    def att_wait_pass(r, e):
+        view, i = att2.at[(1 - yh) * 4 + lax.rem(x + 4 - e, 4), half[r]], 5 + 3 * r + e
+        remote(view, view, att_ss.at[2, i], att_rs.at[2, i], sibling).wait_recv()
 
     def merge(h):
         o_copy(h).wait_recv()
@@ -308,7 +317,10 @@
             att[h, x] = attended
         else:
             att2[t] = attended
-        for e in (1, 3, 2) if h < 2 else (4, 1, 3, 2):
+        if h == 2:
+            go(att_cross, 0)
+            go(att_cross, 1)
+        for e in (1, 3, 2):
             go(att_copy, h, e)
 
     def project(g):
@@ -330,49 +342,52 @@
     def sum_copy():
         return remote(sum_out, sum_in, sum_ss.at[0], sum_rs.at[0], yo)
 
-    for i in (0, 1):
-        go(tok_copy, t, i, yo, 4 + i)
-        go(tok_copy, t, i, xr, 0 + i)
-        go(tok_copy, t, i, xl, 2 + i)
+    for q in (0, 1):
+        go(tok_copy, t, q, xr, L)
+        go(tok_copy, t, 3 - q, xl, R)
+    for q in range(4):
+        go(tok_copy, t, q, yo, Y)
     for u in range(4):
         own(u)
     stats(t, 0)
-    tok_wait(slot_l, 0, 0)
-    go(tok_copy, slot_l, 0, xr, 6)
-    tok_wait(slot_y, 0, 4)
-    go(tok_copy, slot_y, 0, xr, 8)
-    go(tok_copy, slot_y, 0, xl, 10)
+    for q in (0, 1):
+        tok_wait(slot_l, q, L)
+        go(tok_copy, slot_l, q, xr, F)
+        tok_wait(slot_r, 3 - q, R)
+        go(tok_copy, slot_r, 3 - q, xl, F)
+    for q in (0, 1):
+        go(tok_copy, t, 3 - q, xr, L)
+        go(tok_copy, t, q, xl, R)
     event(0, 1)
-    tok_wait(slot_r, 1, 3)
-    go(tok_copy, slot_r, 1, xl, 7)
-    tok_wait(slot_y, 1, 5)
-    go(tok_copy, slot_y, 1, xr, 9)
-    go(tok_copy, slot_y, 1, xl, 11)
+    for q in range(4):
+        tok_wait(slot_y, q, Y)
+        go(tok_copy, slot_y, q, xr, YL)
+        go(tok_copy, slot_y, q, xl, YR)
     event(1, 1)
     event(2, 1)
-    tok_wait(slot_l, 1, 1)
-    tok_wait(slot_r, 0, 2)
-    tok_wait(slot_f, 0, 6)
-    go(tok_copy, slot_f, 0, yo, 12)
-    tok_wait(slot_f, 1, 7)
-    go(tok_copy, slot_f, 1, yo, 13)
+    for q in (0, 3, 1, 2):
+        tok_wait(slot_f, q, F)
+        go(tok_copy, slot_f, q, yo, YF)
     event(3, 1)
     own(4)
     own(5)
+    for q in (0, 1):
+        tok_wait(slot_l, 3 - q, L)
+        tok_wait(slot_r, q, R)
     stats(slot_l, 1)
     stats(slot_r, 2)
     stats(slot_y, 3)
     stats(slot_f, 4)
     event(0, 2)
     event(1, 2)
-    for i in (0, 1):
-        tok_wait(slot_yl, i, 8 + i)
-        tok_wait(slot_yr, i, 10 + i)
+    for q in range(4):
+        tok_wait(slot_yl, q, YL)
+        tok_wait(slot_yr, q, YR)
     stats(slot_yl, 5)
     stats(slot_yr, 6)
     event(2, 2)
-    tok_wait(slot_yf, 0, 12)
-    tok_wait(slot_yf, 1, 13)
+    for q in (0, 3, 1, 2):
+        tok_wait(slot_yf, q, YF)
     stats(slot_yf, 7)
     for g in (0, 1):
         wo_near_own(g).start()
@@ -439,8 +454,8 @@
         (2, 3, 0): [lambda: give(0), lambda: event(5, 3)],
         (2, 4, 0): [lambda: give(1), wo_pass],
         (2, 5, 0): [wo_pass2],
-        (2, 6, 0): [lambda: event(4, 4), lambda: merge(0)],
-        (2, 7, 0): [lambda: merge(1), lambda: event(5, 4)],
+        (2, 6, 0): [lambda: event(4, 4)],
+        (2, 7, 0): [lambda: event(5, 4), lambda: merge(0), lambda: merge(1)],
     }
     groups = [0, 5, 10, 12, 14, 16, 18, 20] + list(range(21, len(order) + 1))
     bufs = (sc_a, sc_b)
@@ -478,17 +493,19 @@
     sum_out[...] = project(1 - yh).astype(BF16)
     go(sum_copy)
     out_ref[...] = project(yh)
-    att_wait(2, 4)
-    for e in (1, 3, 2):
-        go(att_pass, e)
+    for r in (0, 1):
+        att_wait_cross(r)
+        for e in (1, 3, 2):
+            go(att_pass, r, e)
     for e in (1, 2, 3):
         att_wait(2, e)
     wo_share2(1 - c).wait_recv()
     sum_copy().wait_recv()
     out_ref[...] += sum_in[...].astype(F32)
     drain()
-    for e in (5, 6, 7):
-        att_wait(2, e)
+    for r in (0, 1):
+        for e in (1, 2, 3):
+            att_wait_pass(r, e)
     out_ref[...] += project_last()
 
 
@@ -535,10 +552,10 @@
             dma((2, 2 * NH, 4)),
             dma((8, 2 * NH)),
             dma((8, 2 * NH)),
-            dma((14,)),
-            dma((14,)),
-            dma((NH, NT)),
-            dma((NH, NT)),
+            dma((28,)),
+            dma((28,)),
+            dma((NH, 12)),
+            dma((NH, 12)),
             dma((NH,)),
             dma((NH,)),
             dma((NH,)),

time: 65.6 us -> 64.1 us (0.977)
  Pallas kernels: 62.3 us -> 60.9 us
    pallas_call x1, Pallas kernels: 62.3 us -> 60.9 us  [block(): pl.pallas_call(kernel, out_shape=jax.ShapeDtypeStruct((ROWS, WIDTH), F32)...]
where the time goes in v4:
time: 64.1 us; the launch traced here: 63.5 us
  Pallas kernels  60.9 us (95%)
  other arithmetic  1.85 us (3%)
  between operations  0.67 us (1%)
    pallas_call x1, Pallas kernels, block(): pl.pallas_call(kernel, out_shape=jax.ShapeDtypeStruct((ROWS, WIDTH), F32)...  60.9 us
    convert_element_type x1, other arithmetic, local(): return ((tokens.astype(F32) + branch).astype(BF16), branch)  1.85 us

profile of v4, /device:TPU:2, one launch (start us, length us, event | category | flops | bytes accessed | tf_op | source)
XLA Modules:
  0.0 63.5 jit_solution(17496286538505788835)
XLA Ops:
  0.6 0.0 copy-start
  0.6 0.0 copy-start.1
  0.7 60.9 %attention_block.1 = f32[256,384]{1,0:T(8,128)} custom-call(bf16[256,384]{1,0:T(8,128)(2,1)} %tok_in.1, f32[1,3072]{1,0:T(1,128)} %bitcast.6, f32[1,3072]{1,0:T(1,128)} %bitcast.7, bf16[3,3072,384]{2,1,0:T(8,128)(2,1)} %bitcast.4, bf16[3,2,64,3072]{3,2,1,0:T(8,128)(2,1)} %bitcast.5, bf16[256,384]{1,0:T(8,128)(2,1)} %sk_in.1, bf16[256,384]{1,0:T(8,128)(2,1)} %sv_in.1), custom_call_target="tpu_custom_call" | custom-call | tf_op jit(solution)/shard_map/attention_block/pallas_call | solution.py:516
  61.6 0.0 copy-done
  61.6 0.0 copy-done.1
  61.6 1.9 %add_convert_fusion = (bf16[256,384]{1,0:T(8,128)(2,1)}, f32[256,384]{1,0:T(8,128)}) fusion(bf16[256,384]{1,0:T(8,128)(2,1)S(1)} %copy-done, f32[256,384]{1,0:T(8,128)} %attention_block.1, f32[384]{0:T(512)S(1)} %copy-done.1), kind=kLoop, calls=%fused_computation | loop fusion | flops 393216 | bytes 1181184 | tf_op jit(solution)/shard_map/convert_element_type | solution.py:592
Async XLA Ops:
  0.6 61.0 %copy-start = (bf16[256,384]{1,0:T(8,128)(2,1)S(1)}, bf16[256,384]{1,0:T(8,128)(2,1)}, u32[]{:S(2)}) copy-start(bf16[256,384]{1,0:T(8,128)(2,1)} %tok_in.1) | copy-start | bytes 589828
  0.6 61.0 %copy-start.1 = (f32[384]{0:T(512)S(1)}, f32[384]{0:T(512)}, u32[]{:S(2)}) copy-start(f32[384]{0:T(512)} %param.11) | copy-start | bytes 4612

commit v5 on v4

--- a/solution.py
+++ b/solution.py
@@ -441,9 +441,8 @@
     due = {
         (0, 0, 0): [lambda: event(0, 3)],
         (0, 0, ROWS): [lambda: query_in(0), lambda: event(1, 3)],
-        (1, 0, 0): [lambda: query_in(1)],
-        (1, 1, 0): [lambda: event(2, 3)],
-        (1, 3, 0): [lambda: event(3, 3)],
+        (1, 0, 0): [lambda: query_in(1), lambda: event(2, 3)],
+        (1, 2, 0): [lambda: event(3, 3)],
         (1, 4, 0): [lambda: event(4, 2)],
         (2, 0, 0): [lambda: query_in(2)],
         (2, 2, 0): [lambda: event(5, 2)],
@@ -451,11 +450,10 @@
         (1, 5, 0): [lambda: event(1, 4)],
         (1, 6, 0): [lambda: event(2, 4)],
         (0, 7, 0): [lambda: event(3, 4), lambda: event(4, 3)],
-        (2, 3, 0): [lambda: give(0), lambda: event(5, 3)],
-        (2, 4, 0): [lambda: give(1), wo_pass],
-        (2, 5, 0): [wo_pass2],
+        (2, 3, 0): [lambda: event(5, 3), lambda: give(0)],
+        (2, 4, 0): [lambda: give(1)],
         (2, 6, 0): [lambda: event(4, 4)],
-        (2, 7, 0): [lambda: event(5, 4), lambda: merge(0), lambda: merge(1)],
+        (2, 7, 0): [lambda: event(5, 4), lambda: merge(0), lambda: merge(1), wo_pass, wo_pass2],
     }
     groups = [0, 5, 10, 12, 14, 16, 18, 20] + list(range(21, len(order) + 1))
     bufs = (sc_a, sc_b)

time: 64.1 us -> 63.9 us (level)
  no operation moved by 1% of the time
where the time goes in v5:
time: 63.9 us; the launch traced here: 63.5 us
  Pallas kernels  60.9 us (95%)
  other arithmetic  1.85 us (3%)
  between operations  0.67 us (1%)
    pallas_call x1, Pallas kernels, block(): pl.pallas_call(kernel, out_shape=jax.ShapeDtypeStruct((ROWS, WIDTH), F32)...  60.9 us
    convert_element_type x1, other arithmetic, local(): return ((tokens.astype(F32) + branch).astype(BF16), branch)  1.85 us

profile of v5, /device:TPU:2, one launch (start us, length us, event | category | flops | bytes accessed | tf_op | source)
XLA Modules:
  0.0 63.5 jit_solution(13741643935108532722)
XLA Ops:
  0.6 0.0 copy-start
  0.6 0.0 copy-start.1
  0.7 60.9 %attention_block.1 = f32[256,384]{1,0:T(8,128)} custom-call(bf16[256,384]{1,0:T(8,128)(2,1)} %tok_in.1, f32[1,3072]{1,0:T(1,128)} %bitcast.6, f32[1,3072]{1,0:T(1,128)} %bitcast.7, bf16[3,3072,384]{2,1,0:T(8,128)(2,1)} %bitcast.4, bf16[3,2,64,3072]{3,2,1,0:T(8,128)(2,1)} %bitcast.5, bf16[256,384]{1,0:T(8,128)(2,1)} %sk_in.1, bf16[256,384]{1,0:T(8,128)(2,1)} %sv_in.1), custom_call_target="tpu_custom_call" | custom-call | tf_op jit(solution)/shard_map/attention_block/pallas_call | solution.py:514
  61.6 0.0 copy-done
  61.6 0.0 copy-done.1
  61.6 1.9 %add_convert_fusion = (bf16[256,384]{1,0:T(8,128)(2,1)}, f32[256,384]{1,0:T(8,128)}) fusion(bf16[256,384]{1,0:T(8,128)(2,1)S(1)} %copy-done, f32[256,384]{1,0:T(8,128)} %attention_block.1, f32[384]{0:T(512)S(1)} %copy-done.1), kind=kLoop, calls=%fused_computation | loop fusion | flops 393216 | bytes 1181184 | tf_op jit(solution)/shard_map/convert_element_type | solution.py:590
Async XLA Ops:
  0.6 61.0 %copy-start = (bf16[256,384]{1,0:T(8,128)(2,1)S(1)}, bf16[256,384]{1,0:T(8,128)(2,1)}, u32[]{:S(2)}) copy-start(bf16[256,384]{1,0:T(8,128)(2,1)} %tok_in.1) | copy-start | bytes 589828
  0.6 61.0 %copy-start.1 = (f32[384]{0:T(512)S(1)}, f32[384]{0:T(512)}, u32[]{:S(2)}) copy-start(f32[384]{0:T(512)} %param.11) | copy-start | bytes 4612
